TPU v7x, 128 devices: a whole 4x4x4 slice. The times are simulated.
128 devices in a mesh: brick: 8 (over y, core), col: 16 (over z, x).
Axes of the slice: x: 4, y: 4, z: 4, core: 2. Of those that a mesh axis runs over, the one named last changes fastest.
Arguments:
- velocity: float32 [3, 256, 512, 128], P(None, 'brick', 'col'), may hold values from -6 to 6
- pressure: float32 [256, 512, 128], P('brick', 'col'), may hold values from -12 to 12
- level_set: float32 [256, 512, 128], P('brick', 'col'), may hold values from -12 to 12
- overset: int32 [256, 512, 128], P('brick', 'col'), may hold values from 0 to 2
- band_count: int32 [8, 16], P('brick', 'col'), may hold values from 1 to 16, 112 in all within a row
- band_ids: int32 [8, 16, 32], P('brick', 'col'), may hold values from 0 to 31, each once within a row
Outputs:
- velocity_star: float32 [3, 256, 512, 128], P(None, 'brick', 'col')
- level_set_new: float32 [256, 512, 128], P('brick', 'col')
Inputs may be any that keep to these rules, and one draw needn't show every extreme that they name: `band_count`: in each brick row the counts over col sum to exactly 7 times the size of col; some device holds exactly 16. `band_ids`: each device's entries are a permutation of its 32 block numbers.
All inputs are finite; a program needn't handle non-finite values.
Results may differ from a plain program's by a relative error of at most 0.0003.
Values sent between devices are 32-bit elements; how exact they have to be, the bound alone decides.
No kernel may reach another device: no remote copies, remote signals or barrier semaphores. Data moves between devices by JAX's collectives and lax.ppermute only.
A program may use at most 320 MiB of HBM per device.

v0:
```python
import functools

import jax
import jax.numpy as jnp
from jax import lax
from jax.experimental import pallas as pl
from jax.experimental.pallas import tpu as pltpu
from jax.sharding import PartitionSpec as P

BS = 16
REINIT = 3
MAXB = 16
RIM = 4
DEEP = 3
SLABS = RIM + 3 * DEEP + 1
CORNER = (DEEP * SLABS + 7) // 8 * 8
LEFT = 8
UNROLL = 52

DT = 0.1
VISC = 0.5
DT_SET = 0.2
TAU = 0.5

F32 = jnp.float32
ANY = pl.BlockSpec(memory_space=pl.ANY)
VM = pl.BlockSpec(memory_space=pltpu.VMEM)
SM = pl.BlockSpec(memory_space=pltpu.SMEM)


def call(kernel, args, outs, name, aliases=None, sems=0, flops=1 << 20):
    specs = {"vmem": VM, "hbm": ANY, "smem": SM}
    spaces = {"vmem": pltpu.VMEM, "hbm": pltpu.HBM}
    operands = [
        pltpu.with_memory_space_constraint(a, spaces[k]) if k in spaces else a for k, a in args
    ]
    shapes = [
        pltpu.VMEM(s, t) if k == "vmem" else jax.ShapeDtypeStruct(s, t) for k, s, t in outs
    ]
    return pl.pallas_call(
        kernel,
        out_shape=shapes,
        in_specs=[specs[k] for k, _ in args],
        out_specs=[specs[k] for k, _, _ in outs],
        input_output_aliases=aliases or {},
        scratch_shapes=[pltpu.SemaphoreType.DMA((sems,))] if sems else [],
        cost_estimate=pl.CostEstimate(
            flops=flops, bytes_accessed=4 << 20, transcendentals=0
        ),
        compiler_params=pltpu.CompilerParams(vmem_limit_bytes=8 << 20),
        name=name,
    )(*operands)


def copies_of(pairs, sems, first=0):
    return [
        pltpu.make_async_copy(s, d, sems.at[first + i]) for i, (s, d) in enumerate(pairs)
    ]


def start_all(copies):
    for copy in copies:
        copy.start()


def wait_all(copies):
    for copy in copies:
        copy.wait()


def sweep(low, high, tiles, cell):
    rows = high - low
    group = max(g for g in range(1, rows + 1) if rows % g == 0 and g * len(tiles) <= UNROLL)

    def some(i, carry):
        for k in range(group):
            for y in tiles:
                cell(low + i * group + k, y)
        return carry

    if group == rows:
        some(0, 0)
    else:
        lax.fori_loop(0, rows // group, some, 0)


def pack_kernel(vel, press, level, overset, x_lo, x_hi, y_lo, y_hi, V, L, R, K, sems):
    size_x, size_y = level.shape[:2]
    inner = pl.ds(RIM, size_x)
    fields = [(level, L)] + [(vel.at[i], V.at[i]) for i in range(3)] + [(press, R)]

    def part(first, count):
        return [
            (a.at[:, pl.ds(first, count)], b.at[inner, pl.ds(LEFT + first, count)])
            for a, b in fields
        ]

    edges = part(0, 8) + part(size_y - 8, 8)
    rest = []
    for out, high in ((x_lo, False), (x_hi, True)):
        def rows(n):
            return pl.ds(size_x - n if high else 0, n)

        rest.append((level.at[rows(RIM)], out.at[pl.ds(0, RIM)]))
        for i in range(3):
            rest.append((vel.at[i, rows(DEEP)], out.at[pl.ds(RIM + i * DEEP, DEEP)]))
        rest.append((press.at[rows(1)], out.at[pl.ds(RIM + 3 * DEEP, 1)]))
    rest += part(8, size_y - 16) + [(overset, K)]
    edges = copies_of(edges, sems)
    rest = copies_of(rest, sems, len(edges))
    start_all(edges + rest)
    wait_all(edges)

    def gather(x, y):
        for out, high in ((y_lo, False), (y_hi, True)):
            row = (x - RIM) * SLABS

            def take(ref, n, place, *lead):
                start = LEFT + (size_y - n if high else 0)
                out[pl.ds(row + place, n), :] = ref[(*lead, x, pl.ds(start, n), slice(None))]

            take(L, RIM, 0)
            for i in range(3):
                take(V, DEEP, RIM + i * DEEP, i)
            take(R, 1, RIM + 3 * DEEP)

    sweep(RIM, RIM + size_x, [0] * 6, lambda x, y: gather(x, y) if y == 0 else None)
    wait_all(rest)


def relay_kernel(after, q_lo, q_hi, z_lo, z_hi, sems):
    rows = q_lo.shape[0]
    pairs = []
    for out, start in ((z_lo, 0), (z_hi, rows - CORNER)):
        for side, q in enumerate((q_lo, q_hi)):
            pairs.append((q.at[pl.ds(start, CORNER)], out.at[side]))
    copies = copies_of(pairs, sems)
    start_all(copies)
    wait_all(copies)


def turn(value):
    return pltpu.roll(value, 1, 1), pltpu.roll(value, value.shape[1] - 1, 1)


def tile(ref, x, y, *lead):
    return ref[(*lead, x, pl.ds(y, 8), slice(None))]


def predict(V, R, K, VS, x, y):
    kinds = tile(K, x - RIM, y - LEFT)
    rm, rp = turn(tile(R, x, y))
    grads = (
        tile(R, x + 1, y) - tile(R, x - 1, y),
        tile(R, x, y + 1) - tile(R, x, y - 1),
        rp - rm,
    )
    speed = [tile(V, x, y, i) for i in range(3)]
    for i in range(3):
        zm, zp = turn(speed[i])
        plus = (tile(V, x + 1, y, i), tile(V, x, y + 1, i), zp)
        minus = (tile(V, x - 1, y, i), tile(V, x, y - 1, i), zm)
        total = (plus[0] + minus[0]) + (plus[1] + minus[1]) + (plus[2] + minus[2])
        conv = (
            speed[0] * (plus[0] - minus[0])
            + speed[1] * (plus[1] - minus[1])
            + speed[2] * (plus[2] - minus[2])
        )
        pred = speed[i] + DT * (VISC * (total - 6.0 * speed[i]) - 0.5 * (conv + grads[i]))
        mean = total * (1.0 / 6.0)
        VS[i, x - RIM, pl.ds(y - LEFT, 8), :] = jnp.where(
            kinds == 1, mean, jnp.where(kinds == 2, 0.0, pred)
        )


def advect(L, V, A, S, x, y):
    c = tile(L, x, y)
    zm, zp = turn(c)
    v = [tile(V, x, y, i) for i in range(3)]
    flux = jnp.maximum(v[0], 0.0) * (c - tile(L, x - 1, y))
    flux += jnp.minimum(v[0], 0.0) * (tile(L, x + 1, y) - c)
    flux += jnp.maximum(v[1], 0.0) * (c - tile(L, x, y - 1))
    flux += jnp.minimum(v[1], 0.0) * (tile(L, x, y + 1) - c)
    flux += jnp.maximum(v[2], 0.0) * (c - zm)
    flux += jnp.minimum(v[2], 0.0) * (zp - c)
    psi = c - DT_SET * flux
    A[x, pl.ds(y, 8), :] = psi
    S[x, pl.ds(y, 8), :] = (TAU * psi) * lax.rsqrt(psi * psi + 1.0)


def evolved(ref, S, x, y):
    c = tile(ref, x, y)
    s = tile(S, x, y)
    zm, zp = turn(c)
    up = s > 0
    g = None
    for m, p in (
        (tile(ref, x - 1, y), tile(ref, x + 1, y)),
        (tile(ref, x, y - 1), tile(ref, x, y + 1)),
        (zm, zp),
    ):
        low = c - jnp.minimum(jnp.minimum(m, p), c)
        high = jnp.maximum(jnp.maximum(m, p), c) - c
        d = jnp.where(up, low, high)
        g = d * d if g is None else g + d * d
    return c - s * (jnp.sqrt(g) - 1.0)


def evolve(source, target, S, x, y):
    target[x, pl.ds(y, 8), :] = evolved(source, S, x, y)


def finish(source, S, L, M, F, size_y, x, y):
    new = evolved(source, S, x, y)
    y0 = max(y, LEFT)
    y1 = min(y + 8, LEFT + size_y)
    wide = size_y // BS
    first = (y0 - LEFT) // BS
    last = (y1 - 1 - LEFT) // BS
    mark = M[(x - RIM) // BS * wide + first]
    if first != last:
        edge = LEFT + last * BS - y
        rows = lax.broadcasted_iota(jnp.int32, mark.shape, 0)
        mark = jnp.where(rows < edge, mark, M[(x - RIM) // BS * wide + last])
    value = jnp.where(mark > 0.5, new, tile(L, x, y))
    F[x - RIM, pl.ds(y0 - LEFT, y1 - y0), :] = value[y0 - y : y1 - y]


def inner_kernel(V, L, R, K, count, ids, VS, A, S, B, C, F, M):
    size_x, size_y, size_z = F.shape
    wide = size_y // BS
    deep = size_z // BS
    lane = lax.broadcasted_iota(jnp.int32, (8, size_z), 1) // BS
    marks = [jnp.zeros((8, size_z), jnp.bool_) for _ in range(size_x // BS * wide)]
    held = count[0, 0]
    for s in range(MAXB):
        block = jnp.where(s < held, ids[0, 0, s], -1)
        marks = [m | (lane == block - k * deep) for k, m in enumerate(marks)]
    for k, m in enumerate(marks):
        M[k] = m.astype(F32)

    core = [LEFT + y for y in range(0, size_y, 8)]
    mid = [LEFT + y for y in range(RIM, size_y - RIM, 8)]
    low, high = RIM, RIM + size_x
    sweep(low + 1, high - 1, core, functools.partial(advect, L, V, A, S))
    sweep(low + 2, high - 2, core, functools.partial(evolve, A, B, S))
    sweep(low + 3, high - 3, core, functools.partial(evolve, B, C, S))
    sweep(low + 4, high - 4, mid, functools.partial(finish, C, S, L, M, F, size_y))
    sweep(low + 1, high - 1, core[1:-1], functools.partial(predict, V, R, K, VS))


def edge_kernel(
    K, M, x_lo, x_hi, q_lo, q_hi, *refs
):
    V, L, R, VS, A, S, B, C, F, star, sems = refs[9:]
    size_x, size_y = F.shape[:2]
    body = pl.ds(LEFT, size_y)
    low, high = RIM, RIM + size_x
    pairs = []
    for side, x in enumerate((x_lo, x_hi)):
        place = high if side else low - RIM
        pairs.append((x.at[pl.ds(0, RIM)], L.at[pl.ds(place, RIM), body]))
        place = high if side else low - DEEP
        for i in range(3):
            pairs.append(
                (x.at[pl.ds(RIM + i * DEEP, DEEP)], V.at[i, pl.ds(place, DEEP), body])
            )
        place = high if side else low - 1
        pairs.append((x.at[pl.ds(RIM + 3 * DEEP, 1)], R.at[pl.ds(place, 1), body]))
    copies = copies_of(pairs, sems)
    start_all(copies)

    def spread(x, y):
        for side, q in enumerate((q_lo, q_hi)):
            fill(L, V, x, side, q, (), (x - RIM) * SLABS, size_y)
            place = LEFT + size_y if side else LEFT - 1
            R[x, pl.ds(place, 1), :] = q[pl.ds((x - RIM) * SLABS + RIM + 3 * DEEP, 1), :]

    sweep(low, high, [0] * 6, lambda x, y: spread(x, y) if y == 0 else None)
    wait_all(copies)

    core = [LEFT + y for y in range(0, size_y, 8)]
    mid = [LEFT + y for y in range(RIM, size_y - RIM, 8)]
    outer = [LEFT - RIM, LEFT + size_y - RIM]
    step = functools.partial(predict, V, R, K, VS)
    sweep(low + 1, high - 1, [core[0], core[-1]], step)
    for x in (low, high - 1):
        for y in core:
            step(x, y)
    out = copies_of([(VS.at[i], star.at[i]) for i in range(3)], sems, len(copies))
    start_all(out)

    def ring(depth, cell):
        sweep(low - depth, high + depth, outer, cell)
        sweep(low - depth, low - depth + 4, mid, cell)
        sweep(high + depth - 4, high + depth, mid, cell)

    ring(3, functools.partial(advect, L, V, A, S))
    ring(2, functools.partial(evolve, A, B, S))
    ring(1, functools.partial(evolve, B, C, S))
    ring(0, functools.partial(finish, C, S, L, M, F, size_y))
    wait_all(out)


def fill(L, V, x, side, ref, lead, first, size_y):
    place = LEFT + size_y if side else LEFT - RIM
    L[x, pl.ds(place, RIM), :] = ref[(*lead, pl.ds(first, RIM), slice(None))]
    place = LEFT + size_y if side else LEFT - DEEP
    for i in range(3):
        V[i, x, pl.ds(place, DEEP), :] = ref[
            (*lead, pl.ds(first + RIM + i * DEEP, DEEP), slice(None))
        ]


def corner_kernel(M, z_lo, z_hi, *refs):
    V, L, A, S, B, C, F, new, sems = refs[7:]
    size_x, size_y = F.shape[:2]
    low, high = RIM, RIM + size_x
    early = copies_of(
        [(F.at[pl.ds(3, size_x - 6)], new.at[pl.ds(3, size_x - 6)])], sems
    )
    start_all(early)
    skipped = CORNER - DEEP * SLABS
    for k in range(DEEP):
        for side in range(2):
            fill(L, V, low - DEEP + k, side, z_lo, (side,), skipped + k * SLABS, size_y)
            fill(L, V, high + k, side, z_hi, (side,), k * SLABS, size_y)

    outer = [LEFT - RIM, LEFT + size_y - RIM]

    def ends(depth, cell):
        rows = 4 if depth else 3
        for k in range(rows):
            for x in (low - depth + k, high + depth - 1 - k):
                for y in outer:
                    cell(x, y)

    ends(3, functools.partial(advect, L, V, A, S))
    ends(2, functools.partial(evolve, A, B, S))
    ends(1, functools.partial(evolve, B, C, S))
    ends(0, functools.partial(finish, C, S, L, M, F, size_y))
    late = copies_of(
        [(F.at[pl.ds(x, 3)], new.at[pl.ds(x, 3)]) for x in (0, size_x - 3)], sems, 1
    )
    start_all(late)
    wait_all(early + late)


def moved(array, axis, step):
    peers = lax.axis_size(axis)
    return lax.ppermute(array, axis, [(i, (i + step) % peers) for i in range(peers)])


def shards(velocity, pressure, level_set, overset, band_count, band_ids):
    size_x, size_y, size_z = level_set.shape
    plain = level_set.shape
    padded = (size_x + 2 * RIM, LEFT + size_y + 8, size_z)
    x_face = (SLABS, size_y, size_z)
    y_face = (size_x * SLABS, size_z)
    marks = (size_x // BS * (size_y // BS), 8, size_z)

    x_low, x_high, y_low, y_high, V, L, R, K = call(
        pack_kernel,
        [("hbm", velocity), ("hbm", pressure), ("hbm", level_set), ("hbm", overset)],
        [("vmem", x_face, F32)] * 2
        + [("vmem", y_face, F32)] * 2
        + [("vmem", (3,) + padded, F32), ("vmem", padded, F32), ("vmem", padded, F32)]
        + [("vmem", plain, jnp.int32)],
        "pack",
        sems=26,
    )
    q_lo = moved(y_high, "col", 1)
    q_hi = moved(y_low, "col", -1)
    x_lo = moved(x_high, "brick", 1)
    x_hi = moved(x_low, "brick", -1)
    VS, A, S, B, C, F, M = call(
        inner_kernel,
        [("vmem", V), ("vmem", L), ("vmem", R), ("vmem", K)]
        + [("smem", band_count), ("smem", band_ids)],
        [("vmem", (3,) + plain, F32)]
        + [("vmem", padded, F32)] * 4
        + [("vmem", plain, F32), ("vmem", marks, F32)],
        "inner",
        flops=60 << 20,
    )
    z_low, z_high = call(
        relay_kernel,
        [("vmem", M), ("vmem", q_lo), ("vmem", q_hi)],
        [("vmem", (2, CORNER, size_z), F32)] * 2,
        "relay",
        sems=4,
    )
    z_lo = moved(z_high, "brick", 1)
    z_hi = moved(z_low, "brick", -1)
    state = [V, L, R, VS, A, S, B, C, F]
    held = [("vmem", K), ("vmem", M)] + [("vmem", a) for a in (x_lo, x_hi, q_lo, q_hi)]
    *state, velocity_star = call(
        edge_kernel,
        held + [("vmem", a) for a in state],
        [("vmem", a.shape, F32) for a in state] + [("hbm", velocity.shape, F32)],
        "edge",
        aliases={len(held) + i: i for i in range(len(state))},
        sems=13,
        flops=60 << 20,
    )
    V, L, R, VS, A, S, B, C, F = state
    state = [V, L, A, S, B, C, F]
    held = [("vmem", M), ("vmem", z_lo), ("vmem", z_hi)]
    *state, level_set_new = call(
        corner_kernel,
        held + [("vmem", a) for a in state],
        [("vmem", a.shape, F32) for a in state] + [("hbm", plain, F32)],
        "corner",
        aliases={len(held) + i: i for i in range(len(state))},
        sems=3,
    )
    return (velocity_star, level_set_new)


def solution(mesh):
    return jax.shard_map(
        shards,
        mesh=mesh,
        in_specs=(
            P(None, "brick", "col", None),
            P("brick", "col", None),
            P("brick", "col", None),
            P("brick", "col", None),
            P("brick", "col"),
            P("brick", "col", None),
        ),
        out_specs=(P(None, "brick", "col", None), P("brick", "col", None)),
        check_vma=False,
    )
```

profile of v0, /device:TPU:0, one launch (start us, length us, event | category | flops | bytes accessed | tf_op | source)
XLA Modules:
  0.0 24.7 jit_solution(15560671041191220831)
XLA Ops:
  0.6 0.0 copy-start
  0.6 2.3 %pack.1 = (f32[14,32,128]{2,1,0:T(8,128)S(1)}, f32[14,32,128]{2,1,0:T(8,128)S(1)}, f32[448,128]{1,0:T(8,128)S(1)}, f32[448,128]{1,0:T(8,128)S(1)}, f32[3,40,48,1...) custom-call(f32[3,32,32,128]{3,2,1,0:T(8,128)} %vel.1, ...), custom_call_target="tpu_custom_call" | custom-call | flops 1048576 | bytes 4194304 | tf_op jit(solution)/shard_map/pack/pallas_call | solution.py:40
  3.0 1.6 %collective-permute-start.2 = (f32[448,128]{1,0:T(8,128)S(1)}, f32[448,128]{1,0:T(8,128)S(1)}, u32[]{:S(2)}, u32[]{:S(2)}) collective-permute-start(f32[448,128]{1,0:T(8,128)S(1)} %get-tuple-element.35), channel_id=1, source_target_pairs={{0,1},{1,2},{2,3},{3,4},{4,5},{5,6},{6,7},{7,8},{8,9},{9,10},{10,1... | collective-permute-start | bytes 688136 | tf_op jit(solution)/shard_map/ppermute | solution.py:351
  4.6 4.8 %collective-permute-start.3 = (f32[448,128]{1,0:T(8,128)S(1)}, f32[448,128]{1,0:T(8,128)S(1)}, u32[]{:S(2)}, u32[]{:S(2)}) collective-permute-start(f32[448,128]{1,0:T(8,128)S(1)} %get-tuple-element.36), channel_id=1, source_target_pairs={{0,15},{1,0},{2,1},{3,2},{4,3},{5,4},{6,5},{7,6},{8,7},{9,8},{10,9... | collective-permute-start | bytes 688136 | tf_op jit(solution)/shard_map/ppermute | solution.py:351
  9.4 0.0 collective-permute-start
  9.4 3.0 %collective-permute-start.1 = (f32[14,32,128]{2,1,0:T(8,128)S(1)}, f32[14,32,128]{2,1,0:T(8,128)S(1)}, u32[]{:S(2)}, u32[]{:S(2)}) collective-permute-start(f32[14,32,128]{2,1,0:T(8,128)S(1)} %get-tuple-element.34), channel_id=1, source_target_pairs={{0,112},{16,0},{32,16},{48,32},{64,48},{80,64},{96,80},{112,96},{1... | collective-permute-start | bytes 688136 | tf_op jit(solution)/shard_map/ppermute | solution.py:351
  13.1 0.0 copy-done
  13.1 3.5 %inner.1 = (f32[3,32,32,128]{3,2,1,0:T(8,128)S(1)}, f32[40,48,128]{2,1,0:T(8,128)S(1)}, f32[40,48,128]{2,1,0:T(8,128)S(1)}, f32[40,48,128]{2,1,0:T(8,128)S(1)}, ...) custom-call(f32[3,40,48,128]{3,2,1,0:T(8,128)S(1)} %get-tuple-element.29.V.refs_0_, ...), custom_call_target="tpu_custom_call" | custom-call | flops 62914560 | bytes 4194304 | tf_op jit(solution)/shard_map/inner/pallas_call | solution.py:40
  16.6 0.0 collective-permute-done.2.q_lo
  16.6 0.0 collective-permute-done.3.q_hi
  16.6 0.2 relay.1
  16.8 0.0 collective-permute-start.4
  16.8 2.9 %collective-permute-start.5 = (f32[2,48,128]{2,1,0:T(8,128)S(1)}, f32[2,48,128]{2,1,0:T(8,128)S(1)}, u32[]{:S(2)}, u32[]{:S(2)}) collective-permute-start(f32[2,48,128]{2,1,0:T(8,128)S(1)} %get-tuple-element.45), channel_id=1, source_target_pairs={{0,112},{16,0},{32,16},{48,32},{64,48},{80,64},{96,80},{112,96},{1... | collective-permute-start | bytes 147464 | tf_op jit(solution)/shard_map/ppermute | solution.py:351
  19.7 0.0 collective-permute-done.x_lo
  19.8 0.0 collective-permute-done.1.x_hi
  19.8 3.9 %edge.1 = (f32[3,40,48,128]{3,2,1,0:T(8,128)S(1)}, f32[40,48,128]{2,1,0:T(8,128)S(1)}, f32[40,48,128]{2,1,0:T(8,128)S(1)}, f32[3,32,32,128]{3,2,1,0:T(8,128)S(1)...) custom-call(s32[32,32,128]{2,1,0:T(8,128)S(1)} %get-tuple-element.28, ...), custom_call_target="tpu_custom_call", output_to_operand_aliasing={{0}: (6, {}), {1}: (7, {}), {2}: (8, {}), {3}: (9, {}), {4}... | custom-call | flops 62914560 | bytes 4194304 | tf_op jit(solution)/shard_map/edge/pallas_call | solution.py:40
  23.7 0.0 collective-permute-done.4.z_lo
  23.7 0.0 collective-permute-done.5.z_hi
  23.7 1.0 %corner.1 = (f32[3,40,48,128]{3,2,1,0:T(8,128)S(1)}, f32[40,48,128]{2,1,0:T(8,128)S(1)}, f32[40,48,128]{2,1,0:T(8,128)S(1)}, f32[40,48,128]{2,1,0:T(8,128)S(1)},...) custom-call(f32[4,8,128]{2,1,0:T(8,128)S(1)} %get-tuple-element.32.M, ...), custom_call_target="tpu_custom_call", output_to_operand_aliasing={{0}: (3, {}), {1}: (4, {}), {2}: (5, {}), {3}: (6, {}), {4}... | custom-call | flops 1048576 | bytes 4194304 | tf_op jit(solution)/shard_map/corner/pallas_call | solution.py:40
Async XLA Ops:
  0.6 12.4 %copy-start = (s32[1,1,32]{2,1,0:T(1,128)S(1)}, s32[1,1,32]{2,1,0:T(1,128)}, u32[]{:S(2)}) copy-start(s32[1,1,32]{2,1,0:T(1,128)} %ids.1) | copy-start | bytes 388
  3.0 13.6 %collective-permute-start.2 = (f32[448,128]{1,0:T(8,128)S(1)}, f32[448,128]{1,0:T(8,128)S(1)}, u32[]{:S(2)}, u32[]{:S(2)}) collective-permute-start(f32[448,128]{1,0:T(8,128)S(1)} %get-tuple-element.35), channel_id=1, source_target_pairs={{0,1},{1,2},{2,3},{3,4},{4,5},{5,6},{6,7},{7,8},{8,9},{9,10},{10,1... | collective-permute-start | bytes 688136 | tf_op jit(solution)/shard_map/ppermute | solution.py:351
  4.6 12.0 %collective-permute-start.3 = (f32[448,128]{1,0:T(8,128)S(1)}, f32[448,128]{1,0:T(8,128)S(1)}, u32[]{:S(2)}, u32[]{:S(2)}) collective-permute-start(f32[448,128]{1,0:T(8,128)S(1)} %get-tuple-element.36), channel_id=1, source_target_pairs={{0,15},{1,0},{2,1},{3,2},{4,3},{5,4},{6,5},{7,6},{8,7},{9,8},{10,9... | collective-permute-start | bytes 688136 | tf_op jit(solution)/shard_map/ppermute | solution.py:351
  9.4 10.3 %collective-permute-start = (f32[14,32,128]{2,1,0:T(8,128)S(1)}, f32[14,32,128]{2,1,0:T(8,128)S(1)}, u32[]{:S(2)}, u32[]{:S(2)}) collective-permute-start(f32[14,32,128]{2,1,0:T(8,128)S(1)} %get-tuple-element.33), channel_id=1, source_target_pairs={{0,16},{16,32},{32,48},{48,64},{64,80},{80,96},{96,112},{112,0},{1... | collective-permute-start | bytes 688136 | tf_op jit(solution)/shard_map/ppermute | solution.py:351
  9.4 10.3 %collective-permute-start.1 = (f32[14,32,128]{2,1,0:T(8,128)S(1)}, f32[14,32,128]{2,1,0:T(8,128)S(1)}, u32[]{:S(2)}, u32[]{:S(2)}) collective-permute-start(f32[14,32,128]{2,1,0:T(8,128)S(1)} %get-tuple-element.34), channel_id=1, source_target_pairs={{0,112},{16,0},{32,16},{48,32},{64,48},{80,64},{96,80},{112,96},{1... | collective-permute-start | bytes 688136 | tf_op jit(solution)/shard_map/ppermute | solution.py:351
  16.8 6.9 %collective-permute-start.4 = (f32[2,48,128]{2,1,0:T(8,128)S(1)}, f32[2,48,128]{2,1,0:T(8,128)S(1)}, u32[]{:S(2)}, u32[]{:S(2)}) collective-permute-start(f32[2,48,128]{2,1,0:T(8,128)S(1)} %get-tuple-element.44), channel_id=1, source_target_pairs={{0,16},{16,32},{32,48},{48,64},{64,80},{80,96},{96,112},{112,0},{1... | collective-permute-start | bytes 147464 | tf_op jit(solution)/shard_map/ppermute | solution.py:351
  16.8 6.9 %collective-permute-start.5 = (f32[2,48,128]{2,1,0:T(8,128)S(1)}, f32[2,48,128]{2,1,0:T(8,128)S(1)}, u32[]{:S(2)}, u32[]{:S(2)}) collective-permute-start(f32[2,48,128]{2,1,0:T(8,128)S(1)} %get-tuple-element.45), channel_id=1, source_target_pairs={{0,112},{16,0},{32,16},{48,32},{64,48},{80,64},{96,80},{112,96},{1... | collective-permute-start | bytes 147464 | tf_op jit(solution)/shard_map/ppermute | solution.py:351
where the time goes:
time: 24.9 us; the launch traced here: 24.7 us
  starting transfers between devices  12.4 us (50%)
  Pallas kernels  11 us (44%)
  between operations  1.37 us (6%)
    ppermute x6, starting transfers between devices, moved(): lax.ppermute(array, axis, [(i, (i + step) % peers) for i in range(peers)])  12.4 us
    pallas_call x5, Pallas kernels, call(): pl.pallas_call(kernel, out_shape=shapes, in_specs=[specs[k] for k, _ in a...  11 us
  transfers between devices with their start and end apart: 6, of which 0 were waited for; matrix products, arithmetic and copies ran while one was open for 0% of the time, Pallas kernels for 31%

commit v1 on v0

--- a/solution.py
+++ b/solution.py
@@ -15,7 +15,7 @@
 SLABS = RIM + 3 * DEEP + 1
 CORNER = (DEEP * SLABS + 7) // 8 * 8
 LEFT = 8
-UNROLL = 52
+UNROLL = 80
 
 DT = 0.1
 VISC = 0.5
@@ -28,7 +28,7 @@
 SM = pl.BlockSpec(memory_space=pltpu.SMEM)
 
 
-def call(kernel, args, outs, name, aliases=None, sems=0, flops=1 << 20):
+def call(kernel, args, outs, name, aliases=None, sems=0, flops=1 << 20, scratch=()):
     specs = {"vmem": VM, "hbm": ANY, "smem": SM}
     spaces = {"vmem": pltpu.VMEM, "hbm": pltpu.HBM}
     operands = [
@@ -43,7 +43,7 @@
         in_specs=[specs[k] for k, _ in args],
         out_specs=[specs[k] for k, _, _ in outs],
         input_output_aliases=aliases or {},
-        scratch_shapes=[pltpu.SemaphoreType.DMA((sems,))] if sems else [],
+        scratch_shapes=list(scratch) + [pltpu.SemaphoreType.DMA((sems,))],
         cost_estimate=pl.CostEstimate(
             flops=flops, bytes_accessed=4 << 20, transcendentals=0
         ),
@@ -84,30 +84,32 @@
         lax.fori_loop(0, rows // group, some, 0)
 
 
-def pack_kernel(vel, press, level, overset, x_lo, x_hi, y_lo, y_hi, V, L, R, K, sems):
+def pack_kernel(vel, press, level, x_lo, x_hi, y_lo, y_hi, V, L, R, sems):
     size_x, size_y = level.shape[:2]
     inner = pl.ds(RIM, size_x)
+    body = pl.ds(LEFT, size_y)
     fields = [(level, L)] + [(vel.at[i], V.at[i]) for i in range(3)] + [(press, R)]
 
-    def part(first, count):
+    def part(first, count, fields):
         return [
             (a.at[:, pl.ds(first, count)], b.at[inner, pl.ds(LEFT + first, count)])
             for a, b in fields
         ]
 
-    edges = part(0, 8) + part(size_y - 8, 8)
-    rest = []
+    edges = part(0, 8, fields) + part(size_y - 8, 8, fields)
+    rest = part(8, size_y - 16, fields[:-1])
+    local = []
     for out, high in ((x_lo, False), (x_hi, True)):
-        def rows(n):
-            return pl.ds(size_x - n if high else 0, n)
-
-        rest.append((level.at[rows(RIM)], out.at[pl.ds(0, RIM)]))
+        def rows(n, first=RIM):
+            return pl.ds(first + (size_x - n if high else 0), n)
+
+        local.append((L.at[rows(RIM), body], out.at[pl.ds(0, RIM)]))
         for i in range(3):
-            rest.append((vel.at[i, rows(DEEP)], out.at[pl.ds(RIM + i * DEEP, DEEP)]))
-        rest.append((press.at[rows(1)], out.at[pl.ds(RIM + 3 * DEEP, 1)]))
-    rest += part(8, size_y - 16) + [(overset, K)]
+            local.append((V.at[i, rows(DEEP), body], out.at[pl.ds(RIM + i * DEEP, DEEP)]))
+        rest.append((press.at[rows(1, 0)], out.at[pl.ds(RIM + 3 * DEEP, 1)]))
     edges = copies_of(edges, sems)
     rest = copies_of(rest, sems, len(edges))
+    local = copies_of(local, sems, len(edges) + len(rest))
     start_all(edges + rest)
     wait_all(edges)
 
@@ -126,6 +128,8 @@
 
     sweep(RIM, RIM + size_x, [0] * 6, lambda x, y: gather(x, y) if y == 0 else None)
     wait_all(rest)
+    start_all(local)
+    wait_all(local)
 
 
 def relay_kernel(after, q_lo, q_hi, z_lo, z_hi, sems):
@@ -166,7 +170,9 @@
             + speed[1] * (plus[1] - minus[1])
             + speed[2] * (plus[2] - minus[2])
         )
-        pred = speed[i] + DT * (VISC * (total - 6.0 * speed[i]) - 0.5 * (conv + grads[i]))
+        pred = (1.0 - 6.0 * DT * VISC) * speed[i] + (
+            DT * VISC * total - 0.5 * DT * (conv + grads[i])
+        )
         mean = total * (1.0 / 6.0)
         VS[i, x - RIM, pl.ds(y - LEFT, 8), :] = jnp.where(
             kinds == 1, mean, jnp.where(kinds == 2, 0.0, pred)
@@ -177,12 +183,14 @@
     c = tile(L, x, y)
     zm, zp = turn(c)
     v = [tile(V, x, y, i) for i in range(3)]
-    flux = jnp.maximum(v[0], 0.0) * (c - tile(L, x - 1, y))
-    flux += jnp.minimum(v[0], 0.0) * (tile(L, x + 1, y) - c)
-    flux += jnp.maximum(v[1], 0.0) * (c - tile(L, x, y - 1))
-    flux += jnp.minimum(v[1], 0.0) * (tile(L, x, y + 1) - c)
-    flux += jnp.maximum(v[2], 0.0) * (c - zm)
-    flux += jnp.minimum(v[2], 0.0) * (zp - c)
+    flux = None
+    for u, m, p in (
+        (v[0], tile(L, x - 1, y), tile(L, x + 1, y)),
+        (v[1], tile(L, x, y - 1), tile(L, x, y + 1)),
+        (v[2], zm, zp),
+    ):
+        term = u * jnp.where(u > 0, c - m, p - c)
+        flux = term if flux is None else flux + term
     psi = c - DT_SET * flux
     A[x, pl.ds(y, 8), :] = psi
     S[x, pl.ds(y, 8), :] = (TAU * psi) * lax.rsqrt(psi * psi + 1.0)
@@ -203,7 +211,7 @@
         high = jnp.maximum(jnp.maximum(m, p), c) - c
         d = jnp.where(up, low, high)
         g = d * d if g is None else g + d * d
-    return c - s * (jnp.sqrt(g) - 1.0)
+    return c - s * (g * lax.rsqrt(g + 1e-30) - 1.0)
 
 
 def evolve(source, target, S, x, y):
@@ -226,8 +234,29 @@
     F[x - RIM, pl.ds(y0 - LEFT, y1 - y0), :] = value[y0 - y : y1 - y]
 
 
-def inner_kernel(V, L, R, K, count, ids, VS, A, S, B, C, F, M):
+def inner_kernel(
+    V, L, press, overset, count, band_ids, _, R, K, VS, A, S, B, C, F, M, ids, sems
+):
     size_x, size_y, size_z = F.shape
+    middle = size_y - 16
+    named = copies_of([(band_ids, ids)], sems)
+    later = copies_of(
+        [
+            (press.at[:, pl.ds(8, middle)], R.at[pl.ds(RIM, size_x), pl.ds(LEFT + 8, middle)]),
+            (overset, K),
+        ],
+        sems,
+        1,
+    )
+    start_all(named + later)
+    core = [LEFT + y for y in range(0, size_y, 8)]
+    mid = [LEFT + y for y in range(RIM, size_y - RIM, 8)]
+    low, high = RIM, RIM + size_x
+    sweep(low + 1, high - 1, core, functools.partial(advect, L, V, A, S))
+    sweep(low + 2, high - 2, core, functools.partial(evolve, A, B, S))
+    sweep(low + 3, high - 3, core, functools.partial(evolve, B, C, S))
+
+    wait_all(named)
     wide = size_y // BS
     deep = size_z // BS
     lane = lax.broadcasted_iota(jnp.int32, (8, size_z), 1) // BS
@@ -239,13 +268,8 @@
     for k, m in enumerate(marks):
         M[k] = m.astype(F32)
 
-    core = [LEFT + y for y in range(0, size_y, 8)]
-    mid = [LEFT + y for y in range(RIM, size_y - RIM, 8)]
-    low, high = RIM, RIM + size_x
-    sweep(low + 1, high - 1, core, functools.partial(advect, L, V, A, S))
-    sweep(low + 2, high - 2, core, functools.partial(evolve, A, B, S))
-    sweep(low + 3, high - 3, core, functools.partial(evolve, B, C, S))
     sweep(low + 4, high - 4, mid, functools.partial(finish, C, S, L, M, F, size_y))
+    wait_all(later)
     sweep(low + 1, high - 1, core[1:-1], functools.partial(predict, V, R, K, VS))
 
 
@@ -359,28 +383,30 @@
     y_face = (size_x * SLABS, size_z)
     marks = (size_x // BS * (size_y // BS), 8, size_z)
 
-    x_low, x_high, y_low, y_high, V, L, R, K = call(
+    x_low, x_high, y_low, y_high, V, L, R = call(
         pack_kernel,
-        [("hbm", velocity), ("hbm", pressure), ("hbm", level_set), ("hbm", overset)],
+        [("hbm", velocity), ("hbm", pressure), ("hbm", level_set)],
         [("vmem", x_face, F32)] * 2
         + [("vmem", y_face, F32)] * 2
-        + [("vmem", (3,) + padded, F32), ("vmem", padded, F32), ("vmem", padded, F32)]
-        + [("vmem", plain, jnp.int32)],
+        + [("vmem", (3,) + padded, F32), ("vmem", padded, F32), ("vmem", padded, F32)],
         "pack",
-        sems=26,
+        sems=24,
     )
     q_lo = moved(y_high, "col", 1)
     q_hi = moved(y_low, "col", -1)
     x_lo = moved(x_high, "brick", 1)
     x_hi = moved(x_low, "brick", -1)
-    VS, A, S, B, C, F, M = call(
+    R, K, VS, A, S, B, C, F, M = call(
         inner_kernel,
-        [("vmem", V), ("vmem", L), ("vmem", R), ("vmem", K)]
-        + [("smem", band_count), ("smem", band_ids)],
-        [("vmem", (3,) + plain, F32)]
+        [("vmem", V), ("vmem", L), ("hbm", pressure), ("hbm", overset)]
+        + [("smem", band_count), ("hbm", band_ids), ("vmem", R)],
+        [("vmem", padded, F32), ("vmem", plain, jnp.int32), ("vmem", (3,) + plain, F32)]
         + [("vmem", padded, F32)] * 4
         + [("vmem", plain, F32), ("vmem", marks, F32)],
         "inner",
+        aliases={6: 0},
+        scratch=[pltpu.SMEM(band_ids.shape, jnp.int32)],
+        sems=3,
         flops=60 << 20,
     )
     z_low, z_high = call(

time: 24.9 us -> 23.8 us (0.956)
  Pallas kernels: 11 us -> 9.85 us
    pallas_call x5, Pallas kernels: 11 us -> 9.85 us  [call(): pl.pallas_call(kernel, out_shape=shapes, in_specs=[specs[k] for k, _ in a...]
  transfers between devices with their start and end apart: 6 -> 6, of which waited for: 0 -> 0; matrix products, arithmetic and copies ran while one was open for 0% -> 0% of each run, Pallas kernels for 31% -> 28%
where the time goes in v1:
time: 23.8 us; the launch traced here: 23.6 us
  starting transfers between devices  12.4 us (52%)
  Pallas kernels  9.85 us (41%)
  between operations  1.36 us (6%)
    ppermute x6, starting transfers between devices, moved(): lax.ppermute(array, axis, [(i, (i + step) % peers) for i in range(peers)])  12.4 us
    pallas_call x5, Pallas kernels, call(): pl.pallas_call(kernel, out_shape=shapes, in_specs=[specs[k] for k, _ in a...  9.85 us
  transfers between devices with their start and end apart: 6, of which 0 were waited for; matrix products, arithmetic and copies ran while one was open for 0% of the time, Pallas kernels for 28%

profile of v1, /device:TPU:0, one launch (start us, length us, event | category | flops | bytes accessed | tf_op | source)
XLA Modules:
  0.0 23.6 jit_solution(1647928224191919168)
XLA Ops:
  0.6 2.3 %pack.1 = (f32[14,32,128]{2,1,0:T(8,128)S(1)}, f32[14,32,128]{2,1,0:T(8,128)S(1)}, f32[448,128]{1,0:T(8,128)S(1)}, f32[448,128]{1,0:T(8,128)S(1)}, f32[3,40,48,1...) custom-call(f32[3,32,32,128]{3,2,1,0:T(8,128)} %vel.1, f32[32,32,128]{2,1,0:T(8,128)} %press.3, ...), custom_call_target="tpu_custom_call" | custom-call | flops 1048576 | bytes 4194304 | tf_op jit(solution)/shard_map/pack/pallas_call | solution.py:40
  2.9 1.6 %collective-permute-start.2 = (f32[448,128]{1,0:T(8,128)S(1)}, f32[448,128]{1,0:T(8,128)S(1)}, u32[]{:S(2)}, u32[]{:S(2)}) collective-permute-start(f32[448,128]{1,0:T(8,128)S(1)} %get-tuple-element.36), channel_id=1, source_target_pairs={{0,1},{1,2},{2,3},{3,4},{4,5},{5,6},{6,7},{7,8},{8,9},{9,10},{10,1... | collective-permute-start | bytes 688136 | tf_op jit(solution)/shard_map/ppermute | solution.py:375
  4.6 4.8 %collective-permute-start.3 = (f32[448,128]{1,0:T(8,128)S(1)}, f32[448,128]{1,0:T(8,128)S(1)}, u32[]{:S(2)}, u32[]{:S(2)}) collective-permute-start(f32[448,128]{1,0:T(8,128)S(1)} %get-tuple-element.37), channel_id=1, source_target_pairs={{0,15},{1,0},{2,1},{3,2},{4,3},{5,4},{6,5},{7,6},{8,7},{9,8},{10,9... | collective-permute-start | bytes 688136 | tf_op jit(solution)/shard_map/ppermute | solution.py:375
  9.4 0.0 collective-permute-start
  9.4 3.0 %collective-permute-start.1 = (f32[14,32,128]{2,1,0:T(8,128)S(1)}, f32[14,32,128]{2,1,0:T(8,128)S(1)}, u32[]{:S(2)}, u32[]{:S(2)}) collective-permute-start(f32[14,32,128]{2,1,0:T(8,128)S(1)} %get-tuple-element.35), channel_id=1, source_target_pairs={{0,112},{16,0},{32,16},{48,32},{64,48},{80,64},{96,80},{112,96},{1... | collective-permute-start | bytes 688136 | tf_op jit(solution)/shard_map/ppermute | solution.py:375
  13.0 2.6 %inner.1 = (f32[40,48,128]{2,1,0:T(8,128)S(1)}, s32[32,32,128]{2,1,0:T(8,128)S(1)}, f32[3,32,32,128]{3,2,1,0:T(8,128)S(1)}, f32[40,48,128]{2,1,0:T(8,128)S(1)}, ...) custom-call(f32[3,40,48,128]{3,2,1,0:T(8,128)S(1)} %get-tuple-elemen, ...), custom_call_target="tpu_custom_call", output_to_operand_aliasing={{0}: (6, {})} | custom-call | flops 62914560 | bytes 4194304 | tf_op jit(solution)/shard_map/inner/pallas_call | solution.py:40
  15.6 0.0 collective-permute-done.2.q_lo
  15.6 0.0 collective-permute-done.3.q_hi
  15.6 0.2 relay.1
  15.8 0.0 collective-permute-start.4
  15.8 2.9 %collective-permute-start.5 = (f32[2,48,128]{2,1,0:T(8,128)S(1)}, f32[2,48,128]{2,1,0:T(8,128)S(1)}, u32[]{:S(2)}, u32[]{:S(2)}) collective-permute-start(f32[2,48,128]{2,1,0:T(8,128)S(1)} %get-tuple-element.47), channel_id=1, source_target_pairs={{0,112},{16,0},{32,16},{48,32},{64,48},{80,64},{96,80},{112,96},{1... | collective-permute-start | bytes 147464 | tf_op jit(solution)/shard_map/ppermute | solution.py:375
  18.8 0.0 collective-permute-done.x_lo
  18.8 0.0 collective-permute-done.1.x_hi
  18.8 3.8 %edge.1 = (f32[3,40,48,128]{3,2,1,0:T(8,128)S(1)}, f32[40,48,128]{2,1,0:T(8,128)S(1)}, f32[40,48,128]{2,1,0:T(8,128)S(1)}, f32[3,32,32,128]{3,2,1,0:T(8,128)S(1)...) custom-call(s32[32,32,128]{2,1,0:T(8,128)S(1)} %get-tuple-element.32, ...), custom_call_target="tpu_custom_call", output_to_operand_aliasing={{0}: (6, {}), {1}: (7, {}), {2}: (8, {}), {3}: (9, {}), {4}... | custom-call | flops 62914560 | bytes 4194304 | tf_op jit(solution)/shard_map/edge/pallas_call | solution.py:40
  22.6 0.0 collective-permute-done.4.z_lo
  22.6 0.0 collective-permute-done.5.z_hi
  22.6 1.0 %corner.1 = (f32[3,40,48,128]{3,2,1,0:T(8,128)S(1)}, f32[40,48,128]{2,1,0:T(8,128)S(1)}, f32[40,48,128]{2,1,0:T(8,128)S(1)}, f32[40,48,128]{2,1,0:T(8,128)S(1)},...) custom-call(f32[4,8,128]{2,1,0:T(8,128)S(1)} %get-tuple-element.33.M, ...), custom_call_target="tpu_custom_call", output_to_operand_aliasing={{0}: (3, {}), {1}: (4, {}), {2}: (5, {}), {3}: (6, {}), {4}... | custom-call | flops 1048576 | bytes 4194304 | tf_op jit(solution)/shard_map/corner/pallas_call | solution.py:40
Async XLA Ops:
  2.9 12.7 %collective-permute-start.2 = (f32[448,128]{1,0:T(8,128)S(1)}, f32[448,128]{1,0:T(8,128)S(1)}, u32[]{:S(2)}, u32[]{:S(2)}) collective-permute-start(f32[448,128]{1,0:T(8,128)S(1)} %get-tuple-element.36), channel_id=1, source_target_pairs={{0,1},{1,2},{2,3},{3,4},{4,5},{5,6},{6,7},{7,8},{8,9},{9,10},{10,1... | collective-permute-start | bytes 688136 | tf_op jit(solution)/shard_map/ppermute | solution.py:375
  4.6 11.0 %collective-permute-start.3 = (f32[448,128]{1,0:T(8,128)S(1)}, f32[448,128]{1,0:T(8,128)S(1)}, u32[]{:S(2)}, u32[]{:S(2)}) collective-permute-start(f32[448,128]{1,0:T(8,128)S(1)} %get-tuple-element.37), channel_id=1, source_target_pairs={{0,15},{1,0},{2,1},{3,2},{4,3},{5,4},{6,5},{7,6},{8,7},{9,8},{10,9... | collective-permute-start | bytes 688136 | tf_op jit(solution)/shard_map/ppermute | solution.py:375
  9.4 9.4 %collective-permute-start = (f32[14,32,128]{2,1,0:T(8,128)S(1)}, f32[14,32,128]{2,1,0:T(8,128)S(1)}, u32[]{:S(2)}, u32[]{:S(2)}) collective-permute-start(f32[14,32,128]{2,1,0:T(8,128)S(1)} %get-tuple-element.34), channel_id=1, source_target_pairs={{0,16},{16,32},{32,48},{48,64},{64,80},{80,96},{96,112},{112,0},{1... | collective-permute-start | bytes 688136 | tf_op jit(solution)/shard_map/ppermute | solution.py:375
  9.4 9.4 %collective-permute-start.1 = (f32[14,32,128]{2,1,0:T(8,128)S(1)}, f32[14,32,128]{2,1,0:T(8,128)S(1)}, u32[]{:S(2)}, u32[]{:S(2)}) collective-permute-start(f32[14,32,128]{2,1,0:T(8,128)S(1)} %get-tuple-element.35), channel_id=1, source_target_pairs={{0,112},{16,0},{32,16},{48,32},{64,48},{80,64},{96,80},{112,96},{1... | collective-permute-start | bytes 688136 | tf_op jit(solution)/shard_map/ppermute | solution.py:375
  15.8 6.8 %collective-permute-start.4 = (f32[2,48,128]{2,1,0:T(8,128)S(1)}, f32[2,48,128]{2,1,0:T(8,128)S(1)}, u32[]{:S(2)}, u32[]{:S(2)}) collective-permute-start(f32[2,48,128]{2,1,0:T(8,128)S(1)} %get-tuple-element.46), channel_id=1, source_target_pairs={{0,16},{16,32},{32,48},{48,64},{64,80},{80,96},{96,112},{112,0},{1... | collective-permute-start | bytes 147464 | tf_op jit(solution)/shard_map/ppermute | solution.py:375
  15.8 6.8 %collective-permute-start.5 = (f32[2,48,128]{2,1,0:T(8,128)S(1)}, f32[2,48,128]{2,1,0:T(8,128)S(1)}, u32[]{:S(2)}, u32[]{:S(2)}) collective-permute-start(f32[2,48,128]{2,1,0:T(8,128)S(1)} %get-tuple-element.47), channel_id=1, source_target_pairs={{0,112},{16,0},{32,16},{48,32},{64,48},{80,64},{96,80},{112,96},{1... | collective-permute-start | bytes 147464 | tf_op jit(solution)/shard_map/ppermute | solution.py:375

commit v2 on v1

--- a/solution.py
+++ b/solution.py
@@ -68,9 +68,9 @@
         copy.wait()
 
 
-def sweep(low, high, tiles, cell):
+def sweep(low, high, tiles, cell, limit=UNROLL):
     rows = high - low
-    group = max(g for g in range(1, rows + 1) if rows % g == 0 and g * len(tiles) <= UNROLL)
+    group = max(g for g in range(1, rows + 1) if rows % g == 0 and g * len(tiles) <= limit)
 
     def some(i, carry):
         for k in range(group):
@@ -84,58 +84,62 @@
         lax.fori_loop(0, rows // group, some, 0)
 
 
-def pack_kernel(vel, press, level, x_lo, x_hi, y_lo, y_hi, V, L, R, sems):
+def odd_brick():
+    return lax.axis_index("brick") % 2
+
+
+def pack_kernel(vel, press, level, x_in, x_out, y_lo, y_hi, V, L, R, sems):
     size_x, size_y = level.shape[:2]
+    odd = odd_brick()
     inner = pl.ds(RIM, size_x)
-    body = pl.ds(LEFT, size_y)
-    fields = [(level, L)] + [(vel.at[i], V.at[i]) for i in range(3)] + [(press, R)]
-
-    def part(first, count, fields):
+
+    def part(first, count):
+        rows, place = pl.ds(first, count), pl.ds(LEFT + first, count)
         return [
-            (a.at[:, pl.ds(first, count)], b.at[inner, pl.ds(LEFT + first, count)])
-            for a, b in fields
+            (level.at[:, rows], L.at[inner, place]),
+            (vel.at[:, :, rows], V.at[:, inner, place]),
+            (press.at[:, rows], R.at[inner, place]),
         ]
 
-    edges = part(0, 8, fields) + part(size_y - 8, 8, fields)
-    rest = part(8, size_y - 16, fields[:-1])
-    local = []
-    for out, high in ((x_lo, False), (x_hi, True)):
-        def rows(n, first=RIM):
-            return pl.ds(first + (size_x - n if high else 0), n)
-
-        local.append((L.at[rows(RIM), body], out.at[pl.ds(0, RIM)]))
+    strips = part(0, 8) + part(size_y - 8, 8)
+    rest = []
+    for out, high in ((x_in, 1 - odd), (x_out, odd)):
+        def rows(n):
+            return pl.ds(high * (size_x - n), n)
+
+        rest.append((level.at[rows(RIM)], out.at[pl.ds(0, RIM)]))
         for i in range(3):
-            local.append((V.at[i, rows(DEEP), body], out.at[pl.ds(RIM + i * DEEP, DEEP)]))
-        rest.append((press.at[rows(1, 0)], out.at[pl.ds(RIM + 3 * DEEP, 1)]))
-    edges = copies_of(edges, sems)
-    rest = copies_of(rest, sems, len(edges))
-    local = copies_of(local, sems, len(edges) + len(rest))
-    start_all(edges + rest)
-    wait_all(edges)
-
-    def gather(x, y):
-        for out, high in ((y_lo, False), (y_hi, True)):
-            row = (x - RIM) * SLABS
-
-            def take(ref, n, place, *lead):
-                start = LEFT + (size_y - n if high else 0)
-                out[pl.ds(row + place, n), :] = ref[(*lead, x, pl.ds(start, n), slice(None))]
-
-            take(L, RIM, 0)
-            for i in range(3):
-                take(V, DEEP, RIM + i * DEEP, i)
-            take(R, 1, RIM + 3 * DEEP)
-
-    sweep(RIM, RIM + size_x, [0] * 6, lambda x, y: gather(x, y) if y == 0 else None)
+            rest.append((vel.at[i, rows(DEEP)], out.at[pl.ds(RIM + i * DEEP, DEEP)]))
+        rest.append((press.at[rows(1)], out.at[pl.ds(RIM + 3 * DEEP, 1)]))
+    rest += part(8, size_y - 16)[:2]
+    strips = copies_of(strips, sems)
+    rest = copies_of(rest, sems, len(strips))
+    start_all(strips + rest)
+
+    def gather(out, high, x, y):
+        row = (x - RIM) * SLABS
+
+        def take(ref, n, place, *lead):
+            start = LEFT + (size_y - n if high else 0)
+            out[pl.ds(row + place, n), :] = ref[(*lead, x, pl.ds(start, n), slice(None))]
+
+        take(L, RIM, 0)
+        for i in range(3):
+            take(V, DEEP, RIM + i * DEEP, i)
+        take(R, 1, RIM + 3 * DEEP)
+
+    for high, out in enumerate((y_lo, y_hi)):
+        wait_all(strips[3 * high : 3 * high + 3])
+        sweep(RIM, RIM + size_x, [0], functools.partial(gather, out, high), 16)
     wait_all(rest)
-    start_all(local)
-    wait_all(local)
-
-
-def relay_kernel(after, q_lo, q_hi, z_lo, z_hi, sems):
+
+
+def relay_kernel(after, q_lo, q_hi, z_in, z_out, sems):
     rows = q_lo.shape[0]
+    odd = odd_brick()
     pairs = []
-    for out, start in ((z_lo, 0), (z_hi, rows - CORNER)):
+    for out, high in ((z_in, 1 - odd), (z_out, odd)):
+        start = pl.multiple_of(high * (rows - CORNER), 8)
         for side, q in enumerate((q_lo, q_hi)):
             pairs.append((q.at[pl.ds(start, CORNER)], out.at[side]))
     copies = copies_of(pairs, sems)
@@ -274,22 +278,23 @@
 
 
 def edge_kernel(
-    K, M, x_lo, x_hi, q_lo, q_hi, *refs
+    K, M, x_in, x_out, q_lo, q_hi, *refs
 ):
     V, L, R, VS, A, S, B, C, F, star, sems = refs[9:]
     size_x, size_y = F.shape[:2]
     body = pl.ds(LEFT, size_y)
     low, high = RIM, RIM + size_x
+    odd = odd_brick()
     pairs = []
-    for side, x in enumerate((x_lo, x_hi)):
-        place = high if side else low - RIM
+    for x, upper in ((x_in, 1 - odd), (x_out, odd)):
+        place = upper * high + (1 - upper) * (low - RIM)
         pairs.append((x.at[pl.ds(0, RIM)], L.at[pl.ds(place, RIM), body]))
-        place = high if side else low - DEEP
+        place = upper * high + (1 - upper) * (low - DEEP)
         for i in range(3):
             pairs.append(
                 (x.at[pl.ds(RIM + i * DEEP, DEEP)], V.at[i, pl.ds(place, DEEP), body])
             )
-        place = high if side else low - 1
+        place = upper * high + (1 - upper) * (low - 1)
         pairs.append((x.at[pl.ds(RIM + 3 * DEEP, 1)], R.at[pl.ds(place, 1), body]))
     copies = copies_of(pairs, sems)
     start_all(copies)
@@ -300,7 +305,7 @@
             place = LEFT + size_y if side else LEFT - 1
             R[x, pl.ds(place, 1), :] = q[pl.ds((x - RIM) * SLABS + RIM + 3 * DEEP, 1), :]
 
-    sweep(low, high, [0] * 6, lambda x, y: spread(x, y) if y == 0 else None)
+    sweep(low, high, [0], spread, 16)
     wait_all(copies)
 
     core = [LEFT + y for y in range(0, size_y, 8)]
@@ -336,7 +341,7 @@
         ]
 
 
-def corner_kernel(M, z_lo, z_hi, *refs):
+def corner_kernel(M, z_in, z_out, *refs):
     V, L, A, S, B, C, F, new, sems = refs[7:]
     size_x, size_y = F.shape[:2]
     low, high = RIM, RIM + size_x
@@ -345,10 +350,13 @@
     )
     start_all(early)
     skipped = CORNER - DEEP * SLABS
-    for k in range(DEEP):
-        for side in range(2):
-            fill(L, V, low - DEEP + k, side, z_lo, (side,), skipped + k * SLABS, size_y)
-            fill(L, V, high + k, side, z_hi, (side,), k * SLABS, size_y)
+    odd = odd_brick()
+    for z, upper in ((z_in, 1 - odd), (z_out, odd)):
+        place = upper * high + (1 - upper) * (low - DEEP)
+        first = (1 - upper) * skipped
+        for k in range(DEEP):
+            for side in range(2):
+                fill(L, V, place + k, side, z, (side,), first + k * SLABS, size_y)
 
     outer = [LEFT - RIM, LEFT + size_y - RIM]
 
@@ -373,6 +381,12 @@
 def moved(array, axis, step):
     peers = lax.axis_size(axis)
     return lax.ppermute(array, axis, [(i, (i + step) % peers) for i in range(peers)])
+
+
+def swapped(array, axis, shift):
+    peers = lax.axis_size(axis)
+    pairs = [(i, (((i + shift) ^ 1) - shift) % peers) for i in range(peers)]
+    return lax.ppermute(array, axis, pairs)
 
 
 def shards(velocity, pressure, level_set, overset, band_count, band_ids):
@@ -383,7 +397,7 @@
     y_face = (size_x * SLABS, size_z)
     marks = (size_x // BS * (size_y // BS), 8, size_z)
 
-    x_low, x_high, y_low, y_high, V, L, R = call(
+    x_in, x_out, y_low, y_high, V, L, R = call(
         pack_kernel,
         [("hbm", velocity), ("hbm", pressure), ("hbm", level_set)],
         [("vmem", x_face, F32)] * 2
@@ -394,8 +408,8 @@
     )
     q_lo = moved(y_high, "col", 1)
     q_hi = moved(y_low, "col", -1)
-    x_lo = moved(x_high, "brick", 1)
-    x_hi = moved(x_low, "brick", -1)
+    x_in = swapped(x_in, "brick", 0)
+    x_out = swapped(x_out, "brick", 1)
     R, K, VS, A, S, B, C, F, M = call(
         inner_kernel,
         [("vmem", V), ("vmem", L), ("hbm", pressure), ("hbm", overset)]
@@ -409,17 +423,17 @@
         sems=3,
         flops=60 << 20,
     )
-    z_low, z_high = call(
+    z_in, z_out = call(
         relay_kernel,
         [("vmem", M), ("vmem", q_lo), ("vmem", q_hi)],
         [("vmem", (2, CORNER, size_z), F32)] * 2,
         "relay",
         sems=4,
     )
-    z_lo = moved(z_high, "brick", 1)
-    z_hi = moved(z_low, "brick", -1)
+    z_in = swapped(z_in, "brick", 0)
+    z_out = swapped(z_out, "brick", 1)
     state = [V, L, R, VS, A, S, B, C, F]
-    held = [("vmem", K), ("vmem", M)] + [("vmem", a) for a in (x_lo, x_hi, q_lo, q_hi)]
+    held = [("vmem", K), ("vmem", M)] + [("vmem", a) for a in (x_in, x_out, q_lo, q_hi)]
     *state, velocity_star = call(
         edge_kernel,
         held + [("vmem", a) for a in state],
@@ -431,7 +445,7 @@
     )
     V, L, R, VS, A, S, B, C, F = state
     state = [V, L, A, S, B, C, F]
-    held = [("vmem", M), ("vmem", z_lo), ("vmem", z_hi)]
+    held = [("vmem", M), ("vmem", z_in), ("vmem", z_out)]
     *state, level_set_new = call(
         corner_kernel,
         held + [("vmem", a) for a in state],

time: 23.8 us -> 22.7 us (0.954)
  Pallas kernels: 9.85 us -> 9.24 us
  starting transfers between devices: 12.4 us -> 11.9 us
    ppermute x6 -> x2, starting transfers between devices: 12.4 us -> 6.47 us  [moved(): lax.ppermute(array, axis, [(i, (i + step) % peers) for i in range(peers)])]
    ppermute x0 -> x4, starting transfers between devices: none -> 5.43 us  [swapped(): return lax.ppermute(array, axis, pairs)]
    pallas_call x5, Pallas kernels: 9.85 us -> 9.24 us  [call(): pl.pallas_call(kernel, out_shape=shapes, in_specs=[specs[k] for k, _ in a...]
  transfers between devices with their start and end apart: 6 -> 6, of which waited for: 0 -> 0; matrix products, arithmetic and copies ran while one was open for 0% -> 0% of each run, Pallas kernels for 28% -> 27%
where the time goes in v2:
time: 22.7 us; the launch traced here: 22.5 us
  starting transfers between devices  11.9 us (52%)
  Pallas kernels  9.24 us (41%)
  between operations  1.36 us (6%)
    pallas_call x5, Pallas kernels, call(): pl.pallas_call(kernel, out_shape=shapes, in_specs=[specs[k] for k, _ in a...  9.24 us
    ppermute x2, starting transfers between devices, moved(): lax.ppermute(array, axis, [(i, (i + step) % peers) for i in range(peers)])  6.47 us
    ppermute x4, starting transfers between devices, swapped(): return lax.ppermute(array, axis, pairs)  5.43 us
  transfers between devices with their start and end apart: 6, of which 0 were waited for; matrix products, arithmetic and copies ran while one was open for 0% of the time, Pallas kernels for 27%

profile of v2, /device:TPU:0, one launch (start us, length us, event | category | flops | bytes accessed | tf_op | source)
XLA Modules:
  0.0 22.5 jit_solution(7942600307124683741)
XLA Ops:
  0.6 2.0 %pack.1 = (f32[14,32,128]{2,1,0:T(8,128)S(1)}, f32[14,32,128]{2,1,0:T(8,128)S(1)}, f32[448,128]{1,0:T(8,128)S(1)}, f32[448,128]{1,0:T(8,128)S(1)}, f32[3,40,48,1...) custom-call(f32[3,32,32,128]{3,2,1,0:T(8,128)} %vel.1, f32[32,32,128]{2,1,0:T(8,128)} %press.3, ...), custom_call_target="tpu_custom_call" | custom-call | flops 1048576 | bytes 4194304 | tf_op jit(solution)/shard_map/pack/pallas_call | solution.py:40
  2.7 1.6 %collective-permute-start.2 = (f32[448,128]{1,0:T(8,128)S(1)}, f32[448,128]{1,0:T(8,128)S(1)}, u32[]{:S(2)}, u32[]{:S(2)}) collective-permute-start(f32[448,128]{1,0:T(8,128)S(1)} %get-tuple-element.36), channel_id=1, source_target_pairs={{0,1},{1,2},{2,3},{3,4},{4,5},{5,6},{6,7},{7,8},{8,9},{9,10},{10,1... | collective-permute-start | bytes 688136 | tf_op jit(solution)/shard_map/ppermute | solution.py:383
  4.3 4.8 %collective-permute-start.3 = (f32[448,128]{1,0:T(8,128)S(1)}, f32[448,128]{1,0:T(8,128)S(1)}, u32[]{:S(2)}, u32[]{:S(2)}) collective-permute-start(f32[448,128]{1,0:T(8,128)S(1)} %get-tuple-element.37), channel_id=1, source_target_pairs={{0,15},{1,0},{2,1},{3,2},{4,3},{5,4},{6,5},{7,6},{8,7},{9,8},{10,9... | collective-permute-start | bytes 688136 | tf_op jit(solution)/shard_map/ppermute | solution.py:383
  9.1 0.0 collective-permute-start
  9.1 3.1 %collective-permute-start.1 = (f32[14,32,128]{2,1,0:T(8,128)S(1)}, f32[14,32,128]{2,1,0:T(8,128)S(1)}, u32[]{:S(2)}, u32[]{:S(2)}) collective-permute-start(f32[14,32,128]{2,1,0:T(8,128)S(1)} %get-tuple-element.35), channel_id=1, source_target_pairs={{0,112},{16,32},{32,16},{48,64},{64,48},{80,96},{96,80},{112,0},{1... | collective-permute-start | bytes 688136 | tf_op jit(solution)/shard_map/ppermute | solution.py:389
  12.9 2.6 %inner.1 = (f32[40,48,128]{2,1,0:T(8,128)S(1)}, s32[32,32,128]{2,1,0:T(8,128)S(1)}, f32[3,32,32,128]{3,2,1,0:T(8,128)S(1)}, f32[40,48,128]{2,1,0:T(8,128)S(1)}, ...) custom-call(f32[3,40,48,128]{3,2,1,0:T(8,128)S(1)} %get-tuple-elemen, ...), custom_call_target="tpu_custom_call", output_to_operand_aliasing={{0}: (6, {})} | custom-call | flops 62914560 | bytes 4194304 | tf_op jit(solution)/shard_map/inner/pallas_call | solution.py:40
  15.5 0.0 collective-permute-done.2.q_lo
  15.5 0.0 collective-permute-done.3.q_hi
  15.5 0.2 relay.1
  15.7 0.1 collective-permute-start.4
  15.8 2.2 %collective-permute-start.5 = (f32[2,48,128]{2,1,0:T(8,128)S(1)}, f32[2,48,128]{2,1,0:T(8,128)S(1)}, u32[]{:S(2)}, u32[]{:S(2)}) collective-permute-start(f32[2,48,128]{2,1,0:T(8,128)S(1)} %get-tuple-element.47), channel_id=1, source_target_pairs={{0,112},{16,32},{32,16},{48,64},{64,48},{80,96},{96,80},{112,0},{1... | collective-permute-start | bytes 147464 | tf_op jit(solution)/shard_map/ppermute | solution.py:389
  18.0 0.0 collective-permute-done.x_in
  18.0 0.0 collective-permute-done.1.x_out
  18.0 3.4 %edge.1 = (f32[3,40,48,128]{3,2,1,0:T(8,128)S(1)}, f32[40,48,128]{2,1,0:T(8,128)S(1)}, f32[40,48,128]{2,1,0:T(8,128)S(1)}, f32[3,32,32,128]{3,2,1,0:T(8,128)S(1)...) custom-call(s32[32,32,128]{2,1,0:T(8,128)S(1)} %get-tuple-element.32, ...), custom_call_target="tpu_custom_call", output_to_operand_aliasing={{0}: (6, {}), {1}: (7, {}), {2}: (8, {}), {3}: (9, {}), {4}... | custom-call | flops 62914560 | bytes 4194304 | tf_op jit(solution)/shard_map/edge/pallas_call | solution.py:40
  21.4 0.0 collective-permute-done.4.z_in
  21.4 0.0 collective-permute-done.5.z_out
  21.4 1.1 %corner.1 = (f32[3,40,48,128]{3,2,1,0:T(8,128)S(1)}, f32[40,48,128]{2,1,0:T(8,128)S(1)}, f32[40,48,128]{2,1,0:T(8,128)S(1)}, f32[40,48,128]{2,1,0:T(8,128)S(1)},...) custom-call(f32[4,8,128]{2,1,0:T(8,128)S(1)} %get-tuple-element.33.M, ...), custom_call_target="tpu_custom_call", output_to_operand_aliasing={{0}: (3, {}), {1}: (4, {}), {2}: (5, {}), {3}: (6, {}), {4}... | custom-call | flops 1048576 | bytes 4194304 | tf_op jit(solution)/shard_map/corner/pallas_call | solution.py:40
Async XLA Ops:
  2.7 12.8 %collective-permute-start.2 = (f32[448,128]{1,0:T(8,128)S(1)}, f32[448,128]{1,0:T(8,128)S(1)}, u32[]{:S(2)}, u32[]{:S(2)}) collective-permute-start(f32[448,128]{1,0:T(8,128)S(1)} %get-tuple-element.36), channel_id=1, source_target_pairs={{0,1},{1,2},{2,3},{3,4},{4,5},{5,6},{6,7},{7,8},{8,9},{9,10},{10,1... | collective-permute-start | bytes 688136 | tf_op jit(solution)/shard_map/ppermute | solution.py:383
  4.3 11.2 %collective-permute-start.3 = (f32[448,128]{1,0:T(8,128)S(1)}, f32[448,128]{1,0:T(8,128)S(1)}, u32[]{:S(2)}, u32[]{:S(2)}) collective-permute-start(f32[448,128]{1,0:T(8,128)S(1)} %get-tuple-element.37), channel_id=1, source_target_pairs={{0,15},{1,0},{2,1},{3,2},{4,3},{5,4},{6,5},{7,6},{8,7},{9,8},{10,9... | collective-permute-start | bytes 688136 | tf_op jit(solution)/shard_map/ppermute | solution.py:383
  9.1 8.9 %collective-permute-start = (f32[14,32,128]{2,1,0:T(8,128)S(1)}, f32[14,32,128]{2,1,0:T(8,128)S(1)}, u32[]{:S(2)}, u32[]{:S(2)}) collective-permute-start(f32[14,32,128]{2,1,0:T(8,128)S(1)} %get-tuple-element.34), channel_id=1, source_target_pairs={{0,16},{16,0},{32,48},{48,32},{64,80},{80,64},{96,112},{112,96},{1... | collective-permute-start | bytes 688136 | tf_op jit(solution)/shard_map/ppermute | solution.py:389
  9.1 8.9 %collective-permute-start.1 = (f32[14,32,128]{2,1,0:T(8,128)S(1)}, f32[14,32,128]{2,1,0:T(8,128)S(1)}, u32[]{:S(2)}, u32[]{:S(2)}) collective-permute-start(f32[14,32,128]{2,1,0:T(8,128)S(1)} %get-tuple-element.35), channel_id=1, source_target_pairs={{0,112},{16,32},{32,16},{48,64},{64,48},{80,96},{96,80},{112,0},{1... | collective-permute-start | bytes 688136 | tf_op jit(solution)/shard_map/ppermute | solution.py:389
  15.7 5.7 %collective-permute-start.4 = (f32[2,48,128]{2,1,0:T(8,128)S(1)}, f32[2,48,128]{2,1,0:T(8,128)S(1)}, u32[]{:S(2)}, u32[]{:S(2)}) collective-permute-start(f32[2,48,128]{2,1,0:T(8,128)S(1)} %get-tuple-element.46), channel_id=1, source_target_pairs={{0,16},{16,0},{32,48},{48,32},{64,80},{80,64},{96,112},{112,96},{1... | collective-permute-start | bytes 147464 | tf_op jit(solution)/shard_map/ppermute | solution.py:389
  15.8 5.6 %collective-permute-start.5 = (f32[2,48,128]{2,1,0:T(8,128)S(1)}, f32[2,48,128]{2,1,0:T(8,128)S(1)}, u32[]{:S(2)}, u32[]{:S(2)}) collective-permute-start(f32[2,48,128]{2,1,0:T(8,128)S(1)} %get-tuple-element.47), channel_id=1, source_target_pairs={{0,112},{16,32},{32,16},{48,64},{64,48},{80,96},{96,80},{112,0},{1... | collective-permute-start | bytes 147464 | tf_op jit(solution)/shard_map/ppermute | solution.py:389

commit v3 on v2

--- a/solution.py
+++ b/solution.py
@@ -13,7 +13,7 @@
 RIM = 4
 DEEP = 3
 SLABS = RIM + 3 * DEEP + 1
-CORNER = (DEEP * SLABS + 7) // 8 * 8
+CORNER = 32
 LEFT = 8
 UNROLL = 80
 
@@ -116,22 +116,49 @@
     rest = copies_of(rest, sems, len(strips))
     start_all(strips + rest)
 
+    def put(out, row, ref, x, y, n, *lead):
+        out[pl.ds(row, n), :] = ref[(*lead, x, pl.ds(LEFT + y, n), slice(None))]
+
     def gather(out, high, x, y):
-        row = (x - RIM) * SLABS
-
-        def take(ref, n, place, *lead):
-            start = LEFT + (size_y - n if high else 0)
-            out[pl.ds(row + place, n), :] = ref[(*lead, x, pl.ds(start, n), slice(None))]
-
-        take(L, RIM, 0)
+        row = 8 * (x - RIM + 1)
+        near = size_y - 1 if high else 0
+        put(out, row, L, x, size_y - 2 if high else 0, 2)
+        first = size_y - 7 if high else -1
+        psi = advected(L, V, x, LEFT + first)
+        place = (size_y - 3 if high else 1) - first
+        out[pl.ds(row + 2, 2), :] = psi[place : place + 2]
         for i in range(3):
-            take(V, DEEP, RIM + i * DEEP, i)
-        take(R, 1, RIM + 3 * DEEP)
+            put(out, row + 4 + i, V, x, near, 1, i)
+        put(out, row + 7, R, x, near, 1)
 
     for high, out in enumerate((y_lo, y_hi)):
         wait_all(strips[3 * high : 3 * high + 3])
         sweep(RIM, RIM + size_x, [0], functools.partial(gather, out, high), 16)
+        for x, near, more in (
+            (RIM, RIM + 1, 0),
+            (RIM + size_x - 1, RIM + size_x - 2, 8 * (size_x + 1)),
+        ):
+            put(out, 8 * (x - RIM + 1) + 2, L, x, size_y - 4 if high else 2, 2)
+            put(out, more, L, near, size_y - 3 if high else 2, 1)
+            for i in range(3):
+                put(out, more + 1 + 2 * i, V, x, size_y - 3 if high else 1, 2, i)
     wait_all(rest)
+
+
+def fill(L, V, x, side, ref, lead, row, size_y):
+    place = LEFT + size_y if side else LEFT - 2
+    L[x, pl.ds(place, 2), :] = ref[(*lead, pl.ds(row, 2), slice(None))]
+    place = LEFT + size_y if side else LEFT - 1
+    for i in range(3):
+        V[i, x, pl.ds(place, 1), :] = ref[(*lead, pl.ds(row + 4 + i, 1), slice(None))]
+
+
+def fill_raw(L, V, x, side, ref, lead, row, more, size_y):
+    place = LEFT + size_y + 2 if side else LEFT - 4
+    L[x, pl.ds(place, 2), :] = ref[(*lead, pl.ds(row + 2, 2), slice(None))]
+    place = LEFT + size_y + 1 if side else LEFT - 3
+    for i in range(3):
+        V[i, x, pl.ds(place, 2), :] = ref[(*lead, pl.ds(more + 1 + 2 * i, 2), slice(None))]
 
 
 def relay_kernel(after, q_lo, q_hi, z_in, z_out, sems):
@@ -183,7 +210,7 @@
         )
 
 
-def advect(L, V, A, S, x, y):
+def advected(L, V, x, y):
     c = tile(L, x, y)
     zm, zp = turn(c)
     v = [tile(V, x, y, i) for i in range(3)]
@@ -195,9 +222,17 @@
     ):
         term = u * jnp.where(u > 0, c - m, p - c)
         flux = term if flux is None else flux + term
-    psi = c - DT_SET * flux
+    return c - DT_SET * flux
+
+
+def scaled_sign(psi):
+    return (TAU * psi) * lax.rsqrt(psi * psi + 1.0)
+
+
+def advect(L, V, A, S, x, y):
+    psi = advected(L, V, x, y)
     A[x, pl.ds(y, 8), :] = psi
-    S[x, pl.ds(y, 8), :] = (TAU * psi) * lax.rsqrt(psi * psi + 1.0)
+    S[x, pl.ds(y, 8), :] = scaled_sign(psi)
 
 
 def evolved(ref, S, x, y):
@@ -300,12 +335,18 @@
     start_all(copies)
 
     def spread(x, y):
+        row = 8 * (x - RIM + 1)
         for side, q in enumerate((q_lo, q_hi)):
-            fill(L, V, x, side, q, (), (x - RIM) * SLABS, size_y)
+            fill(L, V, x, side, q, (), row, size_y)
             place = LEFT + size_y if side else LEFT - 1
-            R[x, pl.ds(place, 1), :] = q[pl.ds((x - RIM) * SLABS + RIM + 3 * DEEP, 1), :]
+            R[x, pl.ds(place, 1), :] = q[pl.ds(row + 7, 1), :]
 
     sweep(low, high, [0], spread, 16)
+    for side, q in enumerate((q_lo, q_hi)):
+        place = LEFT + size_y + 2 if side else LEFT - 3
+        for x, near, more in ((low, low + 1, 0), (high - 1, high - 2, 8 * (size_x + 1))):
+            fill_raw(L, V, x, side, q, (), 8 * (x - RIM + 1), more, size_y)
+            L[near, pl.ds(place, 1), :] = q[pl.ds(more, 1), :]
     wait_all(copies)
 
     core = [LEFT + y for y in range(0, size_y, 8)]
@@ -325,20 +366,19 @@
         sweep(high + depth - 4, high + depth, mid, cell)
 
     ring(3, functools.partial(advect, L, V, A, S))
+
+    def take(x, y):
+        for side, q in enumerate((q_lo, q_hi)):
+            psi = q[pl.ds(8 * (x - RIM + 1) + 2, 2), :]
+            place = pl.ds(LEFT + size_y + 1 if side else LEFT - 3, 2)
+            A[x, place, :] = psi
+            S[x, place, :] = scaled_sign(psi)
+
+    sweep(low + 1, high - 1, [0], take, 16)
     ring(2, functools.partial(evolve, A, B, S))
     ring(1, functools.partial(evolve, B, C, S))
     ring(0, functools.partial(finish, C, S, L, M, F, size_y))
     wait_all(out)
-
-
-def fill(L, V, x, side, ref, lead, first, size_y):
-    place = LEFT + size_y if side else LEFT - RIM
-    L[x, pl.ds(place, RIM), :] = ref[(*lead, pl.ds(first, RIM), slice(None))]
-    place = LEFT + size_y if side else LEFT - DEEP
-    for i in range(3):
-        V[i, x, pl.ds(place, DEEP), :] = ref[
-            (*lead, pl.ds(first + RIM + i * DEEP, DEEP), slice(None))
-        ]
 
 
 def corner_kernel(M, z_in, z_out, *refs):
@@ -349,14 +389,17 @@
         [(F.at[pl.ds(3, size_x - 6)], new.at[pl.ds(3, size_x - 6)])], sems
     )
     start_all(early)
-    skipped = CORNER - DEEP * SLABS
     odd = odd_brick()
     for z, upper in ((z_in, 1 - odd), (z_out, odd)):
         place = upper * high + (1 - upper) * (low - DEEP)
-        first = (1 - upper) * skipped
-        for k in range(DEEP):
-            for side in range(2):
-                fill(L, V, place + k, side, z, (side,), first + k * SLABS, size_y)
+        edge = upper * high + (1 - upper) * (low - 1)
+        first = upper * 8
+        for side in range(2):
+            for k in range(DEEP):
+                fill(L, V, place + k, side, z, (side,), first + k * 8, size_y)
+            fill_raw(
+                L, V, edge, side, z, (side,), 16 - upper * 8, 24 - upper * 24, size_y
+            )
 
     outer = [LEFT - RIM, LEFT + size_y - RIM]
 
@@ -394,7 +437,7 @@
     plain = level_set.shape
     padded = (size_x + 2 * RIM, LEFT + size_y + 8, size_z)
     x_face = (SLABS, size_y, size_z)
-    y_face = (size_x * SLABS, size_z)
+    y_face = ((size_x + 2) * 8, size_z)
     marks = (size_x // BS * (size_y // BS), 8, size_z)
 
     x_in, x_out, y_low, y_high, V, L, R = call(

time: 22.7 us -> 21.7 us (0.956)
  starting transfers between devices: 11.9 us -> 10.6 us
  waiting for transfers between devices: 0.02 us -> 0.69 us
  Pallas kernels: 9.24 us -> 8.73 us
    ppermute x4, starting transfers between devices: 5.43 us -> 4.39 us  [swapped(): return lax.ppermute(array, axis, pairs)]
    ppermute x4, waiting for transfers between devices: 0.01 us -> 0.68 us  [swapped(): return lax.ppermute(array, axis, pairs)]
    pallas_call x5, Pallas kernels: 9.24 us -> 8.73 us  [call(): pl.pallas_call(kernel, out_shape=shapes, in_specs=[specs[k] for k, _ in a...]
    ppermute x2, starting transfers between devices: 6.47 us -> 6.23 us  [moved(): lax.ppermute(array, axis, [(i, (i + step) % peers) for i in range(peers)])]
  transfers between devices with their start and end apart: 6 -> 6, of which waited for: 0 -> 1; matrix products, arithmetic and copies ran while one was open for 0% -> 0% of each run, Pallas kernels for 27% -> 26%
where the time goes in v3:
time: 21.7 us; the launch traced here: 21.4 us
  starting transfers between devices  10.6 us (49%)
  Pallas kernels  8.73 us (40%)
  between operations  1.36 us (6%)
  waiting for transfers between devices  0.69 us (3%)
    pallas_call x5, Pallas kernels, call(): pl.pallas_call(kernel, out_shape=shapes, in_specs=[specs[k] for k, _ in a...  8.73 us
    ppermute x2, starting transfers between devices, moved(): lax.ppermute(array, axis, [(i, (i + step) % peers) for i in range(peers)])  6.23 us
    ppermute x4, starting transfers between devices, swapped(): return lax.ppermute(array, axis, pairs)  4.39 us
    ppermute x4, waiting for transfers between devices, swapped(): return lax.ppermute(array, axis, pairs)  0.68 us
  transfers between devices with their start and end apart: 6, of which 1 were waited for; matrix products, arithmetic and copies ran while one was open for 0% of the time, Pallas kernels for 26%

profile of v3, /device:TPU:0, one launch (start us, length us, event | category | flops | bytes accessed | tf_op | source)
XLA Modules:
  0.0 21.4 jit_solution(4692575509441747180)
XLA Ops:
  0.6 2.0 %pack.1 = (f32[14,32,128]{2,1,0:T(8,128)S(1)}, f32[14,32,128]{2,1,0:T(8,128)S(1)}, f32[272,128]{1,0:T(8,128)S(1)}, f32[272,128]{1,0:T(8,128)S(1)}, f32[3,40,48,1...) custom-call(f32[3,32,32,128]{3,2,1,0:T(8,128)} %vel.1, f32[32,32,128]{2,1,0:T(8,128)} %press.3, ...), custom_call_target="tpu_custom_call" | custom-call | flops 1048576 | bytes 4194304 | tf_op jit(solution)/shard_map/pack/pallas_call | solution.py:40
  2.7 0.1 collective-permute-start
  2.8 3.2 %collective-permute-start.1 = (f32[14,32,128]{2,1,0:T(8,128)S(1)}, f32[14,32,128]{2,1,0:T(8,128)S(1)}, u32[]{:S(2)}, u32[]{:S(2)}) collective-permute-start(f32[14,32,128]{2,1,0:T(8,128)S(1)} %get-tuple-element.35), channel_id=1, source_target_pairs={{0,112},{16,32},{32,16},{48,64},{64,48},{80,96},{96,80},{112,0},{1... | collective-permute-start | bytes 688136 | tf_op jit(solution)/shard_map/ppermute | solution.py:432
  6.0 1.5 %collective-permute-start.2 = (f32[272,128]{1,0:T(8,128)S(1)}, f32[272,128]{1,0:T(8,128)S(1)}, u32[]{:S(2)}, u32[]{:S(2)}) collective-permute-start(f32[272,128]{1,0:T(8,128)S(1)} %get-tuple-element.36), channel_id=1, source_target_pairs={{0,1},{1,2},{2,3},{3,4},{4,5},{5,6},{6,7},{7,8},{8,9},{9,10},{10,1... | collective-permute-start | bytes 417800 | tf_op jit(solution)/shard_map/ppermute | solution.py:426
  7.5 4.7 %collective-permute-start.3 = (f32[272,128]{1,0:T(8,128)S(1)}, f32[272,128]{1,0:T(8,128)S(1)}, u32[]{:S(2)}, u32[]{:S(2)}) collective-permute-start(f32[272,128]{1,0:T(8,128)S(1)} %get-tuple-element.37), channel_id=1, source_target_pairs={{0,15},{1,0},{2,1},{3,2},{4,3},{5,4},{6,5},{7,6},{8,7},{9,8},{10,9... | collective-permute-start | bytes 417800 | tf_op jit(solution)/shard_map/ppermute | solution.py:426
  12.9 2.6 %inner.1 = (f32[40,48,128]{2,1,0:T(8,128)S(1)}, s32[32,32,128]{2,1,0:T(8,128)S(1)}, f32[3,32,32,128]{3,2,1,0:T(8,128)S(1)}, f32[40,48,128]{2,1,0:T(8,128)S(1)}, ...) custom-call(f32[3,40,48,128]{3,2,1,0:T(8,128)S(1)} %get-tuple-elemen, ...), custom_call_target="tpu_custom_call", output_to_operand_aliasing={{0}: (6, {})} | custom-call | flops 62914560 | bytes 4194304 | tf_op jit(solution)/shard_map/inner/pallas_call | solution.py:40
  15.5 0.0 collective-permute-done.2.q_lo
  15.5 0.0 collective-permute-done.3.q_hi
  15.5 0.1 relay.1
  15.6 0.1 collective-permute-start.4
  15.7 1.0 %collective-permute-start.5 = (f32[2,32,128]{2,1,0:T(8,128)S(1)}, f32[2,32,128]{2,1,0:T(8,128)S(1)}, u32[]{:S(2)}, u32[]{:S(2)}) collective-permute-start(f32[2,32,128]{2,1,0:T(8,128)S(1)} %get-tuple-element.47), channel_id=1, source_target_pairs={{0,112},{16,32},{32,16},{48,64},{64,48},{80,96},{96,80},{112,0},{1... | collective-permute-start | bytes 98312 | tf_op jit(solution)/shard_map/ppermute | solution.py:432
  16.7 0.0 collective-permute-done.x_in
  16.7 0.0 collective-permute-done.1.x_out
  16.8 2.9 %edge.1 = (f32[3,40,48,128]{3,2,1,0:T(8,128)S(1)}, f32[40,48,128]{2,1,0:T(8,128)S(1)}, f32[40,48,128]{2,1,0:T(8,128)S(1)}, f32[3,32,32,128]{3,2,1,0:T(8,128)S(1)...) custom-call(s32[32,32,128]{2,1,0:T(8,128)S(1)} %get-tuple-element.32, ...), custom_call_target="tpu_custom_call", output_to_operand_aliasing={{0}: (6, {}), {1}: (7, {}), {2}: (8, {}), {3}: (9, {}), {4}... | custom-call | flops 62914560 | bytes 4194304 | tf_op jit(solution)/shard_map/edge/pallas_call | solution.py:40
  19.7 0.0 collective-permute-done.4.z_in
  19.7 0.7 %collective-permute-done.5.z_out = f32[2,32,128]{2,1,0:T(8,128)S(1)} collective-permute-done((f32[2,32,128]{2,1,0:T(8,128)S(1)}, f32[2,32,128]{2,1,0:T(8,128)S(1)}, u32[]{:S(2)}, u32[]{:S(2)}) %collective-permute-start.5) | collective-permute-done | bytes 32800 | tf_op jit(solution)/shard_map/ppermute | solution.py:432
  20.4 1.0 %corner.1 = (f32[3,40,48,128]{3,2,1,0:T(8,128)S(1)}, f32[40,48,128]{2,1,0:T(8,128)S(1)}, f32[40,48,128]{2,1,0:T(8,128)S(1)}, f32[40,48,128]{2,1,0:T(8,128)S(1)},...) custom-call(f32[4,8,128]{2,1,0:T(8,128)S(1)} %get-tuple-element.33.M, ...), custom_call_target="tpu_custom_call", output_to_operand_aliasing={{0}: (3, {}), {1}: (4, {}), {2}: (5, {}), {3}: (6, {}), {4}... | custom-call | flops 1048576 | bytes 4194304 | tf_op jit(solution)/shard_map/corner/pallas_call | solution.py:40
Async XLA Ops:
  2.7 14.1 %collective-permute-start = (f32[14,32,128]{2,1,0:T(8,128)S(1)}, f32[14,32,128]{2,1,0:T(8,128)S(1)}, u32[]{:S(2)}, u32[]{:S(2)}) collective-permute-start(f32[14,32,128]{2,1,0:T(8,128)S(1)} %get-tuple-element.34), channel_id=1, source_target_pairs={{0,16},{16,0},{32,48},{48,32},{64,80},{80,64},{96,112},{112,96},{1... | collective-permute-start | bytes 688136 | tf_op jit(solution)/shard_map/ppermute | solution.py:432
  2.8 14.0 %collective-permute-start.1 = (f32[14,32,128]{2,1,0:T(8,128)S(1)}, f32[14,32,128]{2,1,0:T(8,128)S(1)}, u32[]{:S(2)}, u32[]{:S(2)}) collective-permute-start(f32[14,32,128]{2,1,0:T(8,128)S(1)} %get-tuple-element.35), channel_id=1, source_target_pairs={{0,112},{16,32},{32,16},{48,64},{64,48},{80,96},{96,80},{112,0},{1... | collective-permute-start | bytes 688136 | tf_op jit(solution)/shard_map/ppermute | solution.py:432
  6.0 9.5 %collective-permute-start.2 = (f32[272,128]{1,0:T(8,128)S(1)}, f32[272,128]{1,0:T(8,128)S(1)}, u32[]{:S(2)}, u32[]{:S(2)}) collective-permute-start(f32[272,128]{1,0:T(8,128)S(1)} %get-tuple-element.36), channel_id=1, source_target_pairs={{0,1},{1,2},{2,3},{3,4},{4,5},{5,6},{6,7},{7,8},{8,9},{9,10},{10,1... | collective-permute-start | bytes 417800 | tf_op jit(solution)/shard_map/ppermute | solution.py:426
  7.5 8.0 %collective-permute-start.3 = (f32[272,128]{1,0:T(8,128)S(1)}, f32[272,128]{1,0:T(8,128)S(1)}, u32[]{:S(2)}, u32[]{:S(2)}) collective-permute-start(f32[272,128]{1,0:T(8,128)S(1)} %get-tuple-element.37), channel_id=1, source_target_pairs={{0,15},{1,0},{2,1},{3,2},{4,3},{5,4},{6,5},{7,6},{8,7},{9,8},{10,9... | collective-permute-start | bytes 417800 | tf_op jit(solution)/shard_map/ppermute | solution.py:426
  15.6 4.0 %collective-permute-start.4 = (f32[2,32,128]{2,1,0:T(8,128)S(1)}, f32[2,32,128]{2,1,0:T(8,128)S(1)}, u32[]{:S(2)}, u32[]{:S(2)}) collective-permute-start(f32[2,32,128]{2,1,0:T(8,128)S(1)} %get-tuple-element.46), channel_id=1, source_target_pairs={{0,16},{16,0},{32,48},{48,32},{64,80},{80,64},{96,112},{112,96},{1... | collective-permute-start | bytes 98312 | tf_op jit(solution)/shard_map/ppermute | solution.py:432
  15.7 4.6 %collective-permute-start.5 = (f32[2,32,128]{2,1,0:T(8,128)S(1)}, f32[2,32,128]{2,1,0:T(8,128)S(1)}, u32[]{:S(2)}, u32[]{:S(2)}) collective-permute-start(f32[2,32,128]{2,1,0:T(8,128)S(1)} %get-tuple-element.47), channel_id=1, source_target_pairs={{0,112},{16,32},{32,16},{48,64},{64,48},{80,96},{96,80},{112,0},{1... | collective-permute-start | bytes 98312 | tf_op jit(solution)/shard_map/ppermute | solution.py:432

commit v4 on v3

--- a/solution.py
+++ b/solution.py
@@ -88,9 +88,8 @@
     return lax.axis_index("brick") % 2
 
 
-def pack_kernel(vel, press, level, x_in, x_out, y_lo, y_hi, V, L, R, sems):
+def pack_kernel(vel, press, level, y_lo, y_hi, V, L, R, sems):
     size_x, size_y = level.shape[:2]
-    odd = odd_brick()
     inner = pl.ds(RIM, size_x)
 
     def part(first, count):
@@ -102,16 +101,7 @@
         ]
 
     strips = part(0, 8) + part(size_y - 8, 8)
-    rest = []
-    for out, high in ((x_in, 1 - odd), (x_out, odd)):
-        def rows(n):
-            return pl.ds(high * (size_x - n), n)
-
-        rest.append((level.at[rows(RIM)], out.at[pl.ds(0, RIM)]))
-        for i in range(3):
-            rest.append((vel.at[i, rows(DEEP)], out.at[pl.ds(RIM + i * DEEP, DEEP)]))
-        rest.append((press.at[rows(1)], out.at[pl.ds(RIM + 3 * DEEP, 1)]))
-    rest += part(8, size_y - 16)[:2]
+    rest = part(8, size_y - 16)[:2]
     strips = copies_of(strips, sems)
     rest = copies_of(rest, sems, len(strips))
     start_all(strips + rest)
@@ -161,14 +151,26 @@
         V[i, x, pl.ds(place, 2), :] = ref[(*lead, pl.ds(more + 1 + 2 * i, 2), slice(None))]
 
 
-def relay_kernel(after, q_lo, q_hi, z_in, z_out, sems):
+def relay_kernel(V, L, R, after, q_lo, q_hi, x_in, x_out, sems):
     rows = q_lo.shape[0]
+    size_y = x_in.shape[1]
+    size_x = L.shape[0] - 2 * RIM
+    body = pl.ds(LEFT, size_y)
     odd = odd_brick()
     pairs = []
-    for out, high in ((z_in, 1 - odd), (z_out, odd)):
+    for out, high in ((x_in, 1 - odd), (x_out, odd)):
+        def edge(n):
+            return pl.ds(RIM + high * (size_x - n), n)
+
+        pairs.append((L.at[edge(RIM), body], out.at[pl.ds(0, RIM)]))
+        for i in range(3):
+            pairs.append((V.at[i, edge(DEEP), body], out.at[pl.ds(RIM + i * DEEP, DEEP)]))
+        pairs.append((R.at[edge(1), body], out.at[pl.ds(SLABS - 1, 1)]))
         start = pl.multiple_of(high * (rows - CORNER), 8)
         for side, q in enumerate((q_lo, q_hi)):
-            pairs.append((q.at[pl.ds(start, CORNER)], out.at[side]))
+            pairs.append(
+                (q.at[pl.ds(start, CORNER)], out.at[SLABS + side, pl.ds(0, CORNER)])
+            )
     copies = copies_of(pairs, sems)
     start_all(copies)
     wait_all(copies)
@@ -312,10 +314,45 @@
     sweep(low + 1, high - 1, core[1:-1], functools.partial(predict, V, R, K, VS))
 
 
-def edge_kernel(
-    K, M, x_in, x_out, q_lo, q_hi, *refs
-):
-    V, L, R, VS, A, S, B, C, F, star, sems = refs[9:]
+def side_kernel(K, M, q_lo, q_hi, *refs):
+    V, L, R, VS, A, S, B, C, F, sems = refs[9:]
+    size_x, size_y = F.shape[:2]
+    low, high = RIM, RIM + size_x
+
+    def spread(x, y):
+        row = 8 * (x - RIM + 1)
+        for side, q in enumerate((q_lo, q_hi)):
+            fill(L, V, x, side, q, (), row, size_y)
+            place = LEFT + size_y if side else LEFT - 1
+            R[x, pl.ds(place, 1), :] = q[pl.ds(row + 7, 1), :]
+
+    sweep(low, high, [0], spread, 16)
+    for side, q in enumerate((q_lo, q_hi)):
+        place = LEFT + size_y + 2 if side else LEFT - 3
+        for x, near, more in ((low, low + 1, 0), (high - 1, high - 2, 8 * (size_x + 1))):
+            fill_raw(L, V, x, side, q, (), 8 * (x - RIM + 1), more, size_y)
+            L[near, pl.ds(place, 1), :] = q[pl.ds(more, 1), :]
+
+    outer = [LEFT - RIM, LEFT + size_y - RIM]
+    sweep(low + 1, high - 1, outer, functools.partial(advect, L, V, A, S))
+
+    def take(x, y):
+        for side, q in enumerate((q_lo, q_hi)):
+            psi = q[pl.ds(8 * (x - RIM + 1) + 2, 2), :]
+            place = pl.ds(LEFT + size_y + 1 if side else LEFT - 3, 2)
+            A[x, place, :] = psi
+            S[x, place, :] = scaled_sign(psi)
+
+    sweep(low + 1, high - 1, [0], take, 16)
+    sweep(low + 2, high - 2, outer, functools.partial(evolve, A, B, S))
+    sweep(low + 3, high - 3, outer, functools.partial(evolve, B, C, S))
+    sweep(low + 4, high - 4, outer, functools.partial(finish, C, S, L, M, F, size_y))
+    ends = [LEFT, LEFT + size_y - 8]
+    sweep(low + 1, high - 1, ends, functools.partial(predict, V, R, K, VS))
+
+
+def last_kernel(K, M, x_in, x_out, *refs):
+    V, L, R, VS, A, S, B, C, F, star, new, sems = refs[9:]
     size_x, size_y = F.shape[:2]
     body = pl.ds(LEFT, size_y)
     low, high = RIM, RIM + size_x
@@ -330,95 +367,52 @@
                 (x.at[pl.ds(RIM + i * DEEP, DEEP)], V.at[i, pl.ds(place, DEEP), body])
             )
         place = upper * high + (1 - upper) * (low - 1)
-        pairs.append((x.at[pl.ds(RIM + 3 * DEEP, 1)], R.at[pl.ds(place, 1), body]))
+        pairs.append((x.at[pl.ds(SLABS - 1, 1)], R.at[pl.ds(place, 1), body]))
+    middle = pl.ds(1, size_x - 2)
+    pairs.append((VS.at[:, middle], star.at[:, middle]))
+    middle = pl.ds(RIM, size_x - 2 * RIM)
+    pairs.append((F.at[middle], new.at[middle]))
     copies = copies_of(pairs, sems)
     start_all(copies)
-
-    def spread(x, y):
-        row = 8 * (x - RIM + 1)
-        for side, q in enumerate((q_lo, q_hi)):
-            fill(L, V, x, side, q, (), row, size_y)
-            place = LEFT + size_y if side else LEFT - 1
-            R[x, pl.ds(place, 1), :] = q[pl.ds(row + 7, 1), :]
-
-    sweep(low, high, [0], spread, 16)
-    for side, q in enumerate((q_lo, q_hi)):
-        place = LEFT + size_y + 2 if side else LEFT - 3
-        for x, near, more in ((low, low + 1, 0), (high - 1, high - 2, 8 * (size_x + 1))):
-            fill_raw(L, V, x, side, q, (), 8 * (x - RIM + 1), more, size_y)
-            L[near, pl.ds(place, 1), :] = q[pl.ds(more, 1), :]
-    wait_all(copies)
-
-    core = [LEFT + y for y in range(0, size_y, 8)]
-    mid = [LEFT + y for y in range(RIM, size_y - RIM, 8)]
-    outer = [LEFT - RIM, LEFT + size_y - RIM]
-    step = functools.partial(predict, V, R, K, VS)
-    sweep(low + 1, high - 1, [core[0], core[-1]], step)
-    for x in (low, high - 1):
-        for y in core:
-            step(x, y)
-    out = copies_of([(VS.at[i], star.at[i]) for i in range(3)], sems, len(copies))
-    start_all(out)
-
-    def ring(depth, cell):
-        sweep(low - depth, high + depth, outer, cell)
-        sweep(low - depth, low - depth + 4, mid, cell)
-        sweep(high + depth - 4, high + depth, mid, cell)
-
-    ring(3, functools.partial(advect, L, V, A, S))
-
-    def take(x, y):
-        for side, q in enumerate((q_lo, q_hi)):
-            psi = q[pl.ds(8 * (x - RIM + 1) + 2, 2), :]
-            place = pl.ds(LEFT + size_y + 1 if side else LEFT - 3, 2)
-            A[x, place, :] = psi
-            S[x, place, :] = scaled_sign(psi)
-
-    sweep(low + 1, high - 1, [0], take, 16)
-    ring(2, functools.partial(evolve, A, B, S))
-    ring(1, functools.partial(evolve, B, C, S))
-    ring(0, functools.partial(finish, C, S, L, M, F, size_y))
-    wait_all(out)
-
-
-def corner_kernel(M, z_in, z_out, *refs):
-    V, L, A, S, B, C, F, new, sems = refs[7:]
-    size_x, size_y = F.shape[:2]
-    low, high = RIM, RIM + size_x
-    early = copies_of(
-        [(F.at[pl.ds(3, size_x - 6)], new.at[pl.ds(3, size_x - 6)])], sems
-    )
-    start_all(early)
-    odd = odd_brick()
-    for z, upper in ((z_in, 1 - odd), (z_out, odd)):
+    wait_all(copies[:-2])
+    for x, upper in ((x_in, 1 - odd), (x_out, odd)):
         place = upper * high + (1 - upper) * (low - DEEP)
         edge = upper * high + (1 - upper) * (low - 1)
         first = upper * 8
         for side in range(2):
+            lead = (SLABS + side,)
             for k in range(DEEP):
-                fill(L, V, place + k, side, z, (side,), first + k * 8, size_y)
-            fill_raw(
-                L, V, edge, side, z, (side,), 16 - upper * 8, 24 - upper * 24, size_y
-            )
-
-    outer = [LEFT - RIM, LEFT + size_y - RIM]
+                fill(L, V, place + k, side, x, lead, first + k * 8, size_y)
+            fill_raw(L, V, edge, side, x, lead, 16 - upper * 8, 24 - upper * 24, size_y)
+
+    for x in (low, high - 1):
+        for y in range(LEFT, LEFT + size_y, 8):
+            predict(V, R, K, VS, x, y)
+    late = copies_of(
+        [(VS.at[:, pl.ds(x, 1)], star.at[:, pl.ds(x, 1)]) for x in (0, size_x - 1)],
+        sems,
+        len(copies),
+    )
+    start_all(late)
+    tiles = range(LEFT - RIM, LEFT + size_y, 8)
 
     def ends(depth, cell):
-        rows = 4 if depth else 3
-        for k in range(rows):
+        for k in range(4):
             for x in (low - depth + k, high + depth - 1 - k):
-                for y in outer:
+                for y in tiles:
                     cell(x, y)
 
     ends(3, functools.partial(advect, L, V, A, S))
     ends(2, functools.partial(evolve, A, B, S))
     ends(1, functools.partial(evolve, B, C, S))
     ends(0, functools.partial(finish, C, S, L, M, F, size_y))
-    late = copies_of(
-        [(F.at[pl.ds(x, 3)], new.at[pl.ds(x, 3)]) for x in (0, size_x - 3)], sems, 1
-    )
-    start_all(late)
-    wait_all(early + late)
+    tail = copies_of(
+        [(F.at[pl.ds(x, RIM)], new.at[pl.ds(x, RIM)]) for x in (0, size_x - RIM)],
+        sems,
+        len(copies) + len(late),
+    )
+    start_all(tail)
+    wait_all(copies[-2:] + late + tail)
 
 
 def moved(array, axis, step):
@@ -436,23 +430,20 @@
     size_x, size_y, size_z = level_set.shape
     plain = level_set.shape
     padded = (size_x + 2 * RIM, LEFT + size_y + 8, size_z)
-    x_face = (SLABS, size_y, size_z)
+    x_face = (SLABS + 2, size_y, size_z)
     y_face = ((size_x + 2) * 8, size_z)
     marks = (size_x // BS * (size_y // BS), 8, size_z)
 
-    x_in, x_out, y_low, y_high, V, L, R = call(
+    y_low, y_high, V, L, R = call(
         pack_kernel,
         [("hbm", velocity), ("hbm", pressure), ("hbm", level_set)],
-        [("vmem", x_face, F32)] * 2
-        + [("vmem", y_face, F32)] * 2
+        [("vmem", y_face, F32)] * 2
         + [("vmem", (3,) + padded, F32), ("vmem", padded, F32), ("vmem", padded, F32)],
         "pack",
-        sems=24,
+        sems=8,
     )
     q_lo = moved(y_high, "col", 1)
     q_hi = moved(y_low, "col", -1)
-    x_in = swapped(x_in, "brick", 0)
-    x_out = swapped(x_out, "brick", 1)
     R, K, VS, A, S, B, C, F, M = call(
         inner_kernel,
         [("vmem", V), ("vmem", L), ("hbm", pressure), ("hbm", overset)]
@@ -466,36 +457,35 @@
         sems=3,
         flops=60 << 20,
     )
-    z_in, z_out = call(
+    x_in, x_out = call(
         relay_kernel,
-        [("vmem", M), ("vmem", q_lo), ("vmem", q_hi)],
-        [("vmem", (2, CORNER, size_z), F32)] * 2,
+        [("vmem", a) for a in (V, L, R, M, q_lo, q_hi)],
+        [("vmem", x_face, F32)] * 2,
         "relay",
-        sems=4,
-    )
-    z_in = swapped(z_in, "brick", 0)
-    z_out = swapped(z_out, "brick", 1)
+        sems=14,
+    )
+    x_in = swapped(x_in, "brick", 0)
+    x_out = swapped(x_out, "brick", 1)
     state = [V, L, R, VS, A, S, B, C, F]
-    held = [("vmem", K), ("vmem", M)] + [("vmem", a) for a in (x_in, x_out, q_lo, q_hi)]
-    *state, velocity_star = call(
-        edge_kernel,
+    held = [("vmem", a) for a in (K, M, q_lo, q_hi)]
+    state = call(
+        side_kernel,
         held + [("vmem", a) for a in state],
-        [("vmem", a.shape, F32) for a in state] + [("hbm", velocity.shape, F32)],
-        "edge",
+        [("vmem", a.shape, F32) for a in state],
+        "side",
         aliases={len(held) + i: i for i in range(len(state))},
-        sems=13,
         flops=60 << 20,
-    )
-    V, L, R, VS, A, S, B, C, F = state
-    state = [V, L, A, S, B, C, F]
-    held = [("vmem", M), ("vmem", z_in), ("vmem", z_out)]
-    *state, level_set_new = call(
-        corner_kernel,
+        sems=1,
+    )
+    held = [("vmem", a) for a in (K, M, x_in, x_out)]
+    *_, velocity_star, level_set_new = call(
+        last_kernel,
         held + [("vmem", a) for a in state],
-        [("vmem", a.shape, F32) for a in state] + [("hbm", plain, F32)],
-        "corner",
+        [("vmem", a.shape, F32) for a in state]
+        + [("hbm", velocity.shape, F32), ("hbm", plain, F32)],
+        "last",
         aliases={len(held) + i: i for i in range(len(state))},
-        sems=3,
+        sems=16,
     )
     return (velocity_star, level_set_new)
 

time: 21.7 us -> 22.6 us (1.041)
  the two profiles are of different devices: /device:TPU:0 before, /device:TPU:25 now
where the time goes in v4:
time: 22.6 us; the launch traced here: 22.5 us
  Pallas kernels  8.39 us (37%)
  starting transfers between devices  7.41 us (33%)
  waiting for transfers between devices  5.36 us (24%)
  between operations  1.32 us (6%)
    pallas_call x5, Pallas kernels, call(): pl.pallas_call(kernel, out_shape=shapes, in_specs=[specs[k] for k, _ in a...  8.39 us
    ppermute x2, starting transfers between devices, moved(): lax.ppermute(array, axis, [(i, (i + step) % peers) for i in range(peers)])  6.1 us
    ppermute x2, waiting for transfers between devices, swapped(): return lax.ppermute(array, axis, pairs)  5.28 us
    ppermute x2, starting transfers between devices, swapped(): return lax.ppermute(array, axis, pairs)  1.31 us
  transfers between devices with their start and end apart: 4, of which 2 were waited for; matrix products, arithmetic and copies ran while one was open for 0% of the time, Pallas kernels for 19%

profile of v4, /device:TPU:25, one launch (start us, length us, event | category | flops | bytes accessed | tf_op | source)
XLA Modules:
  0.0 22.5 jit_solution(8893683388025433791)
XLA Ops:
  0.6 1.7 %pack.1 = (f32[272,128]{1,0:T(8,128)S(1)}, f32[272,128]{1,0:T(8,128)S(1)}, f32[3,40,48,128]{3,2,1,0:T(8,128)S(1)}, f32[40,48,128]{2,1,0:T(8,128)S(1)}, f32[40,48,128]{2,1,0:T(8,128)S(1)}) custom-call(f32[3,32,32,128]{3,2,1,0:T(8,128)} %vel.1, f32[32,32,128]{2,1,0:T(8,128)} %press.3, f32[32,32,128]{2,1,0:T(8,128)} %level.1), custom_call_target="tpu_custom_call" | custom-call | flops 1048576 | bytes 4194304 | tf_op jit(solution)/shard_map/pack/pallas_call | solution.py:40
  2.4 1.3 %collective-permute-start = (f32[272,128]{1,0:T(8,128)S(1)}, f32[272,128]{1,0:T(8,128)S(1)}, u32[]{:S(2)}, u32[]{:S(2)}) collective-permute-start(f32[272,128]{1,0:T(8,128)S(1)} %get-tuple-element.35), channel_id=1, source_target_pairs={{0,1},{1,2},{2,3},{3,4},{4,5},{5,6},{6,7},{7,8},{8,9},{9,10},{10,1... | collective-permute-start | bytes 417800 | tf_op jit(solution)/shard_map/ppermute | solution.py:420
  3.7 4.8 %collective-permute-start.1 = (f32[272,128]{1,0:T(8,128)S(1)}, f32[272,128]{1,0:T(8,128)S(1)}, u32[]{:S(2)}, u32[]{:S(2)}) collective-permute-start(f32[272,128]{1,0:T(8,128)S(1)} %get-tuple-element.36), channel_id=1, source_target_pairs={{0,15},{1,0},{2,1},{3,2},{4,3},{5,4},{6,5},{7,6},{8,7},{9,8},{10,9... | collective-permute-start | bytes 417800 | tf_op jit(solution)/shard_map/ppermute | solution.py:420
  9.1 2.6 %inner.1 = (f32[40,48,128]{2,1,0:T(8,128)S(1)}, s32[32,32,128]{2,1,0:T(8,128)S(1)}, f32[3,32,32,128]{3,2,1,0:T(8,128)S(1)}, f32[40,48,128]{2,1,0:T(8,128)S(1)}, ...) custom-call(f32[3,40,48,128]{3,2,1,0:T(8,128)S(1)} %get-tuple-elemen, ...), custom_call_target="tpu_custom_call", output_to_operand_aliasing={{0}: (6, {})} | custom-call | flops 62914560 | bytes 4194304 | tf_op jit(solution)/shard_map/inner/pallas_call | solution.py:40
  11.7 0.1 collective-permute-done.q_lo
  11.8 0.0 collective-permute-done.1.q_hi
  11.8 0.4 %relay.1 = (f32[16,32,128]{2,1,0:T(8,128)S(1)}, f32[16,32,128]{2,1,0:T(8,128)S(1)}) custom-call(f32[3,40,48,128]{3,2,1,0:T(8,128)S(1)} %get-tuple-element.29.V.refs_0_, f32[40,48,128]{2,1,0:T(8,128)S(1)} %get-tuple-element.30.L.refs_1_, f32[40,48,128]{2,1,0:T(8,128)S(1)} %get-tuple-element.34.R.refs_2_, f32[4,8,128]{2,1,0:T(8,128)S(1)} %get-tuple-element.33.after.M, ...), custom_call_target="tpu_custom_call" | custom-call | flops 1048576 | bytes 4194304 | tf_op jit(solution)/shard_map/relay/pallas_call | solution.py:40
  12.3 1.3 %collective-permute-start.2 = (f32[16,32,128]{2,1,0:T(8,128)S(1)}, f32[16,32,128]{2,1,0:T(8,128)S(1)}, u32[]{:S(2)}, u32[]{:S(2)}) collective-permute-start(f32[16,32,128]{2,1,0:T(8,128)S(1)} %get-tuple-element.37), channel_id=1, source_target_pairs={{0,16},{16,0},{32,48},{48,32},{64,80},{80,64},{96,112},{112,96},{1... | collective-permute-start | bytes 786440 | tf_op jit(solution)/shard_map/ppermute | solution.py:426
  13.6 0.0 collective-permute-start.3
  13.6 1.7 %side.1 = (f32[3,40,48,128]{3,2,1,0:T(8,128)S(1)}, f32[40,48,128]{2,1,0:T(8,128)S(1)}, f32[40,48,128]{2,1,0:T(8,128)S(1)}, f32[3,32,32,128]{3,2,1,0:T(8,128)S(1)...) custom-call(s32[32,32,128]{2,1,0:T(8,128)S(1)} %get-tuple-element.32, ...), custom_call_target="tpu_custom_call", output_to_operand_aliasing={{0}: (4, {}), {1}: (5, {}), {2}: (6, {}), {3}: (7, {}), {4}... | custom-call | flops 62914560 | bytes 4194304 | tf_op jit(solution)/shard_map/side/pallas_call | solution.py:40
  15.3 0.0 collective-permute-done.2.x_in
  15.3 5.3 %collective-permute-done.3.x_out = f32[16,32,128]{2,1,0:T(8,128)S(1)} collective-permute-done((f32[16,32,128]{2,1,0:T(8,128)S(1)}, f32[16,32,128]{2,1,0:T(8,128)S(1)}, u32[]{:S(2)}, u32[]{:S(2)}) %collective-permute-start.3) | collective-permute-done | bytes 262176 | tf_op jit(solution)/shard_map/ppermute | solution.py:426
  20.6 1.9 %last.1 = (f32[3,40,48,128]{3,2,1,0:T(8,128)S(1)}, f32[40,48,128]{2,1,0:T(8,128)S(1)}, f32[40,48,128]{2,1,0:T(8,128)S(1)}, f32[3,32,32,128]{3,2,1,0:T(8,128)S(1)...) custom-call(s32[32,32,128]{2,1,0:T(8,128)S(1)} %get-tuple-element.32, ...), custom_call_target="tpu_custom_call", output_to_operand_aliasing={{0}: (4, {}), {1}: (5, {}), {2}: (6, {}), {3}: (7, {}), {4}... | custom-call | flops 1048576 | bytes 4194304 | tf_op jit(solution)/shard_map/last/pallas_call | solution.py:40
Async XLA Ops:
  2.4 9.4 %collective-permute-start = (f32[272,128]{1,0:T(8,128)S(1)}, f32[272,128]{1,0:T(8,128)S(1)}, u32[]{:S(2)}, u32[]{:S(2)}) collective-permute-start(f32[272,128]{1,0:T(8,128)S(1)} %get-tuple-element.35), channel_id=1, source_target_pairs={{0,1},{1,2},{2,3},{3,4},{4,5},{5,6},{6,7},{7,8},{8,9},{9,10},{10,1... | collective-permute-start | bytes 417800 | tf_op jit(solution)/shard_map/ppermute | solution.py:420
  3.7 8.1 %collective-permute-start.1 = (f32[272,128]{1,0:T(8,128)S(1)}, f32[272,128]{1,0:T(8,128)S(1)}, u32[]{:S(2)}, u32[]{:S(2)}) collective-permute-start(f32[272,128]{1,0:T(8,128)S(1)} %get-tuple-element.36), channel_id=1, source_target_pairs={{0,15},{1,0},{2,1},{3,2},{4,3},{5,4},{6,5},{7,6},{8,7},{9,8},{10,9... | collective-permute-start | bytes 417800 | tf_op jit(solution)/shard_map/ppermute | solution.py:420
  12.3 3.0 %collective-permute-start.2 = (f32[16,32,128]{2,1,0:T(8,128)S(1)}, f32[16,32,128]{2,1,0:T(8,128)S(1)}, u32[]{:S(2)}, u32[]{:S(2)}) collective-permute-start(f32[16,32,128]{2,1,0:T(8,128)S(1)} %get-tuple-element.37), channel_id=1, source_target_pairs={{0,16},{16,0},{32,48},{48,32},{64,80},{80,64},{96,112},{112,96},{1... | collective-permute-start | bytes 786440 | tf_op jit(solution)/shard_map/ppermute | solution.py:426
  13.6 7.0 %collective-permute-start.3 = (f32[16,32,128]{2,1,0:T(8,128)S(1)}, f32[16,32,128]{2,1,0:T(8,128)S(1)}, u32[]{:S(2)}, u32[]{:S(2)}) collective-permute-start(f32[16,32,128]{2,1,0:T(8,128)S(1)} %get-tuple-element.38), channel_id=1, source_target_pairs={{0,112},{16,32},{32,16},{48,64},{64,48},{80,96},{96,80},{112,0},{1... | collective-permute-start | bytes 786440 | tf_op jit(solution)/shard_map/ppermute | solution.py:426

commit v5 on v3

--- a/solution.py
+++ b/solution.py
@@ -464,7 +464,7 @@
         aliases={6: 0},
         scratch=[pltpu.SMEM(band_ids.shape, jnp.int32)],
         sems=3,
-        flops=60 << 20,
+        flops=60 << 26,
     )
     z_in, z_out = call(
         relay_kernel,
@@ -484,7 +484,7 @@
         "edge",
         aliases={len(held) + i: i for i in range(len(state))},
         sems=13,
-        flops=60 << 20,
+        flops=60 << 26,
     )
     V, L, R, VS, A, S, B, C, F = state
     state = [V, L, A, S, B, C, F]

time: 21.7 us -> 21.7 us (level)
  waiting for transfers between devices: 0.69 us -> 0.92 us
    ppermute x4, starting transfers between devices: 4.39 us -> 4.06 us  [swapped(): return lax.ppermute(array, axis, pairs)]
    ppermute x2, starting transfers between devices: 6.23 us -> 6.47 us  [moved(): lax.ppermute(array, axis, [(i, (i + step) % peers) for i in range(peers)])]
    ppermute x4, waiting for transfers between devices: 0.68 us -> 0.91 us  [swapped(): return lax.ppermute(array, axis, pairs)]
where the time goes in v5:
time: 21.7 us; the launch traced here: 21.4 us
  starting transfers between devices  10.5 us (48%)
  Pallas kernels  8.6 us (40%)
  between operations  1.35 us (6%)
  waiting for transfers between devices  0.92 us (4%)
    pallas_call x5, Pallas kernels, call(): pl.pallas_call(kernel, out_shape=shapes, in_specs=[specs[k] for k, _ in a...  8.6 us
    ppermute x2, starting transfers between devices, moved(): lax.ppermute(array, axis, [(i, (i + step) % peers) for i in range(peers)])  6.47 us
    ppermute x4, starting transfers between devices, swapped(): return lax.ppermute(array, axis, pairs)  4.06 us
    ppermute x4, waiting for transfers between devices, swapped(): return lax.ppermute(array, axis, pairs)  0.91 us
  transfers between devices with their start and end apart: 6, of which 1 were waited for; matrix products, arithmetic and copies ran while one was open for 0% of the time, Pallas kernels for 26%

profile of v5, /device:TPU:0, one launch (start us, length us, event | category | flops | bytes accessed | tf_op | source)
XLA Modules:
  0.0 21.4 jit_solution(3565593718999295708)
XLA Ops:
  0.6 2.0 %pack.1 = (f32[14,32,128]{2,1,0:T(8,128)S(1)}, f32[14,32,128]{2,1,0:T(8,128)S(1)}, f32[272,128]{1,0:T(8,128)S(1)}, f32[272,128]{1,0:T(8,128)S(1)}, f32[3,40,48,1...) custom-call(f32[3,32,32,128]{3,2,1,0:T(8,128)} %vel.1, f32[32,32,128]{2,1,0:T(8,128)} %press.3, ...), custom_call_target="tpu_custom_call" | custom-call | flops 1048576 | bytes 4194304 | tf_op jit(solution)/shard_map/pack/pallas_call | solution.py:40
  2.7 1.6 %collective-permute-start.2 = (f32[272,128]{1,0:T(8,128)S(1)}, f32[272,128]{1,0:T(8,128)S(1)}, u32[]{:S(2)}, u32[]{:S(2)}) collective-permute-start(f32[272,128]{1,0:T(8,128)S(1)} %get-tuple-element.36), channel_id=1, source_target_pairs={{0,1},{1,2},{2,3},{3,4},{4,5},{5,6},{6,7},{7,8},{8,9},{9,10},{10,1... | collective-permute-start | bytes 417800 | tf_op jit(solution)/shard_map/ppermute | solution.py:426
  4.3 4.8 %collective-permute-start.3 = (f32[272,128]{1,0:T(8,128)S(1)}, f32[272,128]{1,0:T(8,128)S(1)}, u32[]{:S(2)}, u32[]{:S(2)}) collective-permute-start(f32[272,128]{1,0:T(8,128)S(1)} %get-tuple-element.37), channel_id=1, source_target_pairs={{0,15},{1,0},{2,1},{3,2},{4,3},{5,4},{6,5},{7,6},{8,7},{9,8},{10,9... | collective-permute-start | bytes 417800 | tf_op jit(solution)/shard_map/ppermute | solution.py:426
  9.1 0.0 collective-permute-start
  9.1 3.1 %collective-permute-start.1 = (f32[14,32,128]{2,1,0:T(8,128)S(1)}, f32[14,32,128]{2,1,0:T(8,128)S(1)}, u32[]{:S(2)}, u32[]{:S(2)}) collective-permute-start(f32[14,32,128]{2,1,0:T(8,128)S(1)} %get-tuple-element.35), channel_id=1, source_target_pairs={{0,112},{16,32},{32,16},{48,64},{64,48},{80,96},{96,80},{112,0},{1... | collective-permute-start | bytes 688136 | tf_op jit(solution)/shard_map/ppermute | solution.py:432
  12.9 2.5 %inner.1 = (f32[40,48,128]{2,1,0:T(8,128)S(1)}, s32[32,32,128]{2,1,0:T(8,128)S(1)}, f32[3,32,32,128]{3,2,1,0:T(8,128)S(1)}, f32[40,48,128]{2,1,0:T(8,128)S(1)}, ...) custom-call(f32[3,40,48,128]{3,2,1,0:T(8,128)S(1)} %get-tuple-elemen, ...), custom_call_target="tpu_custom_call", output_to_operand_aliasing={{0}: (6, {})} | custom-call | flops 4026531840 | bytes 4194304 | tf_op jit(solution)/shard_map/inner/pallas_call | solution.py:40
  15.5 0.0 collective-permute-done.2.q_lo
  15.5 0.0 collective-permute-done.3.q_hi
  15.5 0.1 relay.1
  15.6 0.1 collective-permute-start.4
  15.7 0.8 %collective-permute-start.5 = (f32[2,32,128]{2,1,0:T(8,128)S(1)}, f32[2,32,128]{2,1,0:T(8,128)S(1)}, u32[]{:S(2)}, u32[]{:S(2)}) collective-permute-start(f32[2,32,128]{2,1,0:T(8,128)S(1)} %get-tuple-element.47), channel_id=1, source_target_pairs={{0,112},{16,32},{32,16},{48,64},{64,48},{80,96},{96,80},{112,0},{1... | collective-permute-start | bytes 98312 | tf_op jit(solution)/shard_map/ppermute | solution.py:432
  16.6 0.0 collective-permute-done.x_in
  16.6 0.0 collective-permute-done.1.x_out
  16.6 2.9 %edge.1 = (f32[3,40,48,128]{3,2,1,0:T(8,128)S(1)}, f32[40,48,128]{2,1,0:T(8,128)S(1)}, f32[40,48,128]{2,1,0:T(8,128)S(1)}, f32[3,32,32,128]{3,2,1,0:T(8,128)S(1)...) custom-call(s32[32,32,128]{2,1,0:T(8,128)S(1)} %get-tuple-element.32, ...), custom_call_target="tpu_custom_call", output_to_operand_aliasing={{0}: (6, {}), {1}: (7, {}), {2}: (8, {}), {3}: (9, {}), {4}... | custom-call | flops 4026531840 | bytes 4194304 | tf_op jit(solution)/shard_map/edge/pallas_call | solution.py:40
  19.4 0.0 collective-permute-done.4.z_in
  19.5 0.9 %collective-permute-done.5.z_out = f32[2,32,128]{2,1,0:T(8,128)S(1)} collective-permute-done((f32[2,32,128]{2,1,0:T(8,128)S(1)}, f32[2,32,128]{2,1,0:T(8,128)S(1)}, u32[]{:S(2)}, u32[]{:S(2)}) %collective-permute-start.5) | collective-permute-done | bytes 32800 | tf_op jit(solution)/shard_map/ppermute | solution.py:432
  20.4 1.0 %corner.1 = (f32[3,40,48,128]{3,2,1,0:T(8,128)S(1)}, f32[40,48,128]{2,1,0:T(8,128)S(1)}, f32[40,48,128]{2,1,0:T(8,128)S(1)}, f32[40,48,128]{2,1,0:T(8,128)S(1)},...) custom-call(f32[4,8,128]{2,1,0:T(8,128)S(1)} %get-tuple-element.33.M, ...), custom_call_target="tpu_custom_call", output_to_operand_aliasing={{0}: (3, {}), {1}: (4, {}), {2}: (5, {}), {3}: (6, {}), {4}... | custom-call | flops 1048576 | bytes 4194304 | tf_op jit(solution)/shard_map/corner/pallas_call | solution.py:40
Async XLA Ops:
  2.7 12.8 %collective-permute-start.2 = (f32[272,128]{1,0:T(8,128)S(1)}, f32[272,128]{1,0:T(8,128)S(1)}, u32[]{:S(2)}, u32[]{:S(2)}) collective-permute-start(f32[272,128]{1,0:T(8,128)S(1)} %get-tuple-element.36), channel_id=1, source_target_pairs={{0,1},{1,2},{2,3},{3,4},{4,5},{5,6},{6,7},{7,8},{8,9},{9,10},{10,1... | collective-permute-start | bytes 417800 | tf_op jit(solution)/shard_map/ppermute | solution.py:426
  4.3 11.2 %collective-permute-start.3 = (f32[272,128]{1,0:T(8,128)S(1)}, f32[272,128]{1,0:T(8,128)S(1)}, u32[]{:S(2)}, u32[]{:S(2)}) collective-permute-start(f32[272,128]{1,0:T(8,128)S(1)} %get-tuple-element.37), channel_id=1, source_target_pairs={{0,15},{1,0},{2,1},{3,2},{4,3},{5,4},{6,5},{7,6},{8,7},{9,8},{10,9... | collective-permute-start | bytes 417800 | tf_op jit(solution)/shard_map/ppermute | solution.py:426
  9.1 7.4 %collective-permute-start = (f32[14,32,128]{2,1,0:T(8,128)S(1)}, f32[14,32,128]{2,1,0:T(8,128)S(1)}, u32[]{:S(2)}, u32[]{:S(2)}) collective-permute-start(f32[14,32,128]{2,1,0:T(8,128)S(1)} %get-tuple-element.34), channel_id=1, source_target_pairs={{0,16},{16,0},{32,48},{48,32},{64,80},{80,64},{96,112},{112,96},{1... | collective-permute-start | bytes 688136 | tf_op jit(solution)/shard_map/ppermute | solution.py:432
  9.1 7.4 %collective-permute-start.1 = (f32[14,32,128]{2,1,0:T(8,128)S(1)}, f32[14,32,128]{2,1,0:T(8,128)S(1)}, u32[]{:S(2)}, u32[]{:S(2)}) collective-permute-start(f32[14,32,128]{2,1,0:T(8,128)S(1)} %get-tuple-element.35), channel_id=1, source_target_pairs={{0,112},{16,32},{32,16},{48,64},{64,48},{80,96},{96,80},{112,0},{1... | collective-permute-start | bytes 688136 | tf_op jit(solution)/shard_map/ppermute | solution.py:432
  15.6 3.8 %collective-permute-start.4 = (f32[2,32,128]{2,1,0:T(8,128)S(1)}, f32[2,32,128]{2,1,0:T(8,128)S(1)}, u32[]{:S(2)}, u32[]{:S(2)}) collective-permute-start(f32[2,32,128]{2,1,0:T(8,128)S(1)} %get-tuple-element.46), channel_id=1, source_target_pairs={{0,16},{16,0},{32,48},{48,32},{64,80},{80,64},{96,112},{112,96},{1... | collective-permute-start | bytes 98312 | tf_op jit(solution)/shard_map/ppermute | solution.py:432
  15.7 4.6 %collective-permute-start.5 = (f32[2,32,128]{2,1,0:T(8,128)S(1)}, f32[2,32,128]{2,1,0:T(8,128)S(1)}, u32[]{:S(2)}, u32[]{:S(2)}) collective-permute-start(f32[2,32,128]{2,1,0:T(8,128)S(1)} %get-tuple-element.47), channel_id=1, source_target_pairs={{0,112},{16,32},{32,16},{48,64},{64,48},{80,96},{96,80},{112,0},{1... | collective-permute-start | bytes 98312 | tf_op jit(solution)/shard_map/ppermute | solution.py:432

commit v6 on v5

--- a/solution.py
+++ b/solution.py
@@ -15,7 +15,7 @@
 SLABS = RIM + 3 * DEEP + 1
 CORNER = 32
 LEFT = 8
-UNROLL = 80
+UNROLL = 120
 
 DT = 0.1
 VISC = 0.5

time: 21.7 us -> 21.5 us (level)
  transfers between devices with their start and end apart: 6 -> 6, of which waited for: 1 -> 1; matrix products, arithmetic and copies ran while one was open for 0% -> 0% of each run, Pallas kernels for 26% -> 25%
where the time goes in v6:
time: 21.5 us; the launch traced here: 21.3 us
  starting transfers between devices  10.5 us (49%)
  Pallas kernels  8.48 us (39%)
  between operations  1.35 us (6%)
  waiting for transfers between devices  0.92 us (4%)
    pallas_call x5, Pallas kernels, call(): pl.pallas_call(kernel, out_shape=shapes, in_specs=[specs[k] for k, _ in a...  8.48 us
    ppermute x2, starting transfers between devices, moved(): lax.ppermute(array, axis, [(i, (i + step) % peers) for i in range(peers)])  6.47 us
    ppermute x4, starting transfers between devices, swapped(): return lax.ppermute(array, axis, pairs)  4.06 us
    ppermute x4, waiting for transfers between devices, swapped(): return lax.ppermute(array, axis, pairs)  0.91 us
  transfers between devices with their start and end apart: 6, of which 1 were waited for; matrix products, arithmetic and copies ran while one was open for 0% of the time, Pallas kernels for 25%

profile of v6, /device:TPU:0, one launch (start us, length us, event | category | flops | bytes accessed | tf_op | source)
XLA Modules:
  0.0 21.3 jit_solution(18270860166431618588)
XLA Ops:
  0.6 2.0 %pack.1 = (f32[14,32,128]{2,1,0:T(8,128)S(1)}, f32[14,32,128]{2,1,0:T(8,128)S(1)}, f32[272,128]{1,0:T(8,128)S(1)}, f32[272,128]{1,0:T(8,128)S(1)}, f32[3,40,48,1...) custom-call(f32[3,32,32,128]{3,2,1,0:T(8,128)} %vel.1, f32[32,32,128]{2,1,0:T(8,128)} %press.3, ...), custom_call_target="tpu_custom_call" | custom-call | flops 1048576 | bytes 4194304 | tf_op jit(solution)/shard_map/pack/pallas_call | solution.py:40
  2.7 1.6 %collective-permute-start.2 = (f32[272,128]{1,0:T(8,128)S(1)}, f32[272,128]{1,0:T(8,128)S(1)}, u32[]{:S(2)}, u32[]{:S(2)}) collective-permute-start(f32[272,128]{1,0:T(8,128)S(1)} %get-tuple-element.36), channel_id=1, source_target_pairs={{0,1},{1,2},{2,3},{3,4},{4,5},{5,6},{6,7},{7,8},{8,9},{9,10},{10,1... | collective-permute-start | bytes 417800 | tf_op jit(solution)/shard_map/ppermute | solution.py:426
  4.3 4.8 %collective-permute-start.3 = (f32[272,128]{1,0:T(8,128)S(1)}, f32[272,128]{1,0:T(8,128)S(1)}, u32[]{:S(2)}, u32[]{:S(2)}) collective-permute-start(f32[272,128]{1,0:T(8,128)S(1)} %get-tuple-element.37), channel_id=1, source_target_pairs={{0,15},{1,0},{2,1},{3,2},{4,3},{5,4},{6,5},{7,6},{8,7},{9,8},{10,9... | collective-permute-start | bytes 417800 | tf_op jit(solution)/shard_map/ppermute | solution.py:426
  9.1 0.0 collective-permute-start
  9.1 3.1 %collective-permute-start.1 = (f32[14,32,128]{2,1,0:T(8,128)S(1)}, f32[14,32,128]{2,1,0:T(8,128)S(1)}, u32[]{:S(2)}, u32[]{:S(2)}) collective-permute-start(f32[14,32,128]{2,1,0:T(8,128)S(1)} %get-tuple-element.35), channel_id=1, source_target_pairs={{0,112},{16,32},{32,16},{48,64},{64,48},{80,96},{96,80},{112,0},{1... | collective-permute-start | bytes 688136 | tf_op jit(solution)/shard_map/ppermute | solution.py:432
  12.9 2.4 %inner.1 = (f32[40,48,128]{2,1,0:T(8,128)S(1)}, s32[32,32,128]{2,1,0:T(8,128)S(1)}, f32[3,32,32,128]{3,2,1,0:T(8,128)S(1)}, f32[40,48,128]{2,1,0:T(8,128)S(1)}, ...) custom-call(f32[3,40,48,128]{3,2,1,0:T(8,128)S(1)} %get-tuple-elemen, ...), custom_call_target="tpu_custom_call", output_to_operand_aliasing={{0}: (6, {})} | custom-call | flops 4026531840 | bytes 4194304 | tf_op jit(solution)/shard_map/inner/pallas_call | solution.py:40
  15.3 0.0 collective-permute-done.2.q_lo
  15.3 0.0 collective-permute-done.3.q_hi
  15.4 0.1 relay.1
  15.5 0.1 collective-permute-start.4
  15.6 0.8 %collective-permute-start.5 = (f32[2,32,128]{2,1,0:T(8,128)S(1)}, f32[2,32,128]{2,1,0:T(8,128)S(1)}, u32[]{:S(2)}, u32[]{:S(2)}) collective-permute-start(f32[2,32,128]{2,1,0:T(8,128)S(1)} %get-tuple-element.47), channel_id=1, source_target_pairs={{0,112},{16,32},{32,16},{48,64},{64,48},{80,96},{96,80},{112,0},{1... | collective-permute-start | bytes 98312 | tf_op jit(solution)/shard_map/ppermute | solution.py:432
  16.4 0.0 collective-permute-done.x_in
  16.4 0.0 collective-permute-done.1.x_out
  16.4 2.9 %edge.1 = (f32[3,40,48,128]{3,2,1,0:T(8,128)S(1)}, f32[40,48,128]{2,1,0:T(8,128)S(1)}, f32[40,48,128]{2,1,0:T(8,128)S(1)}, f32[3,32,32,128]{3,2,1,0:T(8,128)S(1)...) custom-call(s32[32,32,128]{2,1,0:T(8,128)S(1)} %get-tuple-element.32, ...), custom_call_target="tpu_custom_call", output_to_operand_aliasing={{0}: (6, {}), {1}: (7, {}), {2}: (8, {}), {3}: (9, {}), {4}... | custom-call | flops 4026531840 | bytes 4194304 | tf_op jit(solution)/shard_map/edge/pallas_call | solution.py:40
  19.3 0.0 collective-permute-done.4.z_in
  19.3 0.9 %collective-permute-done.5.z_out = f32[2,32,128]{2,1,0:T(8,128)S(1)} collective-permute-done((f32[2,32,128]{2,1,0:T(8,128)S(1)}, f32[2,32,128]{2,1,0:T(8,128)S(1)}, u32[]{:S(2)}, u32[]{:S(2)}) %collective-permute-start.5) | collective-permute-done | bytes 32800 | tf_op jit(solution)/shard_map/ppermute | solution.py:432
  20.2 1.0 %corner.1 = (f32[3,40,48,128]{3,2,1,0:T(8,128)S(1)}, f32[40,48,128]{2,1,0:T(8,128)S(1)}, f32[40,48,128]{2,1,0:T(8,128)S(1)}, f32[40,48,128]{2,1,0:T(8,128)S(1)},...) custom-call(f32[4,8,128]{2,1,0:T(8,128)S(1)} %get-tuple-element.33.M, ...), custom_call_target="tpu_custom_call", output_to_operand_aliasing={{0}: (3, {}), {1}: (4, {}), {2}: (5, {}), {3}: (6, {}), {4}... | custom-call | flops 1048576 | bytes 4194304 | tf_op jit(solution)/shard_map/corner/pallas_call | solution.py:40
Async XLA Ops:
  2.7 12.7 %collective-permute-start.2 = (f32[272,128]{1,0:T(8,128)S(1)}, f32[272,128]{1,0:T(8,128)S(1)}, u32[]{:S(2)}, u32[]{:S(2)}) collective-permute-start(f32[272,128]{1,0:T(8,128)S(1)} %get-tuple-element.36), channel_id=1, source_target_pairs={{0,1},{1,2},{2,3},{3,4},{4,5},{5,6},{6,7},{7,8},{8,9},{9,10},{10,1... | collective-permute-start | bytes 417800 | tf_op jit(solution)/shard_map/ppermute | solution.py:426
  4.3 11.0 %collective-permute-start.3 = (f32[272,128]{1,0:T(8,128)S(1)}, f32[272,128]{1,0:T(8,128)S(1)}, u32[]{:S(2)}, u32[]{:S(2)}) collective-permute-start(f32[272,128]{1,0:T(8,128)S(1)} %get-tuple-element.37), channel_id=1, source_target_pairs={{0,15},{1,0},{2,1},{3,2},{4,3},{5,4},{6,5},{7,6},{8,7},{9,8},{10,9... | collective-permute-start | bytes 417800 | tf_op jit(solution)/shard_map/ppermute | solution.py:426
  9.1 7.3 %collective-permute-start = (f32[14,32,128]{2,1,0:T(8,128)S(1)}, f32[14,32,128]{2,1,0:T(8,128)S(1)}, u32[]{:S(2)}, u32[]{:S(2)}) collective-permute-start(f32[14,32,128]{2,1,0:T(8,128)S(1)} %get-tuple-element.34), channel_id=1, source_target_pairs={{0,16},{16,0},{32,48},{48,32},{64,80},{80,64},{96,112},{112,96},{1... | collective-permute-start | bytes 688136 | tf_op jit(solution)/shard_map/ppermute | solution.py:432
  9.1 7.3 %collective-permute-start.1 = (f32[14,32,128]{2,1,0:T(8,128)S(1)}, f32[14,32,128]{2,1,0:T(8,128)S(1)}, u32[]{:S(2)}, u32[]{:S(2)}) collective-permute-start(f32[14,32,128]{2,1,0:T(8,128)S(1)} %get-tuple-element.35), channel_id=1, source_target_pairs={{0,112},{16,32},{32,16},{48,64},{64,48},{80,96},{96,80},{112,0},{1... | collective-permute-start | bytes 688136 | tf_op jit(solution)/shard_map/ppermute | solution.py:432
  15.5 3.8 %collective-permute-start.4 = (f32[2,32,128]{2,1,0:T(8,128)S(1)}, f32[2,32,128]{2,1,0:T(8,128)S(1)}, u32[]{:S(2)}, u32[]{:S(2)}) collective-permute-start(f32[2,32,128]{2,1,0:T(8,128)S(1)} %get-tuple-element.46), channel_id=1, source_target_pairs={{0,16},{16,0},{32,48},{48,32},{64,80},{80,64},{96,112},{112,96},{1... | collective-permute-start | bytes 98312 | tf_op jit(solution)/shard_map/ppermute | solution.py:432
  15.6 4.6 %collective-permute-start.5 = (f32[2,32,128]{2,1,0:T(8,128)S(1)}, f32[2,32,128]{2,1,0:T(8,128)S(1)}, u32[]{:S(2)}, u32[]{:S(2)}) collective-permute-start(f32[2,32,128]{2,1,0:T(8,128)S(1)} %get-tuple-element.47), channel_id=1, source_target_pairs={{0,112},{16,32},{32,16},{48,64},{64,48},{80,96},{96,80},{112,0},{1... | collective-permute-start | bytes 98312 | tf_op jit(solution)/shard_map/ppermute | solution.py:432

commit v7 on v6

--- a/solution.py
+++ b/solution.py
@@ -133,7 +133,7 @@
 
     for high, out in enumerate((y_lo, y_hi)):
         wait_all(strips[3 * high : 3 * high + 3])
-        sweep(RIM, RIM + size_x, [0], functools.partial(gather, out, high), 16)
+        sweep(RIM, RIM + size_x, [0], functools.partial(gather, out, high), 32)
         for x, near, more in (
             (RIM, RIM + 1, 0),
             (RIM + size_x - 1, RIM + size_x - 2, 8 * (size_x + 1)),
@@ -341,7 +341,7 @@
             place = LEFT + size_y if side else LEFT - 1
             R[x, pl.ds(place, 1), :] = q[pl.ds(row + 7, 1), :]
 
-    sweep(low, high, [0], spread, 16)
+    sweep(low, high, [0], spread, 32)
     for side, q in enumerate((q_lo, q_hi)):
         place = LEFT + size_y + 2 if side else LEFT - 3
         for x, near, more in ((low, low + 1, 0), (high - 1, high - 2, 8 * (size_x + 1))):
@@ -374,7 +374,7 @@
             A[x, place, :] = psi
             S[x, place, :] = scaled_sign(psi)
 
-    sweep(low + 1, high - 1, [0], take, 16)
+    sweep(low + 1, high - 1, [0], take, 32)
     ring(2, functools.partial(evolve, A, B, S))
     ring(1, functools.partial(evolve, B, C, S))
     ring(0, functools.partial(finish, C, S, L, M, F, size_y))

time: 21.5 us -> 21.7 us (level)
  waiting for transfers between devices: 0.92 us -> 0.4 us
  Pallas kernels: 8.48 us -> 8.99 us
    ppermute x4, waiting for transfers between devices: 0.91 us -> 0.4 us  [swapped(): return lax.ppermute(array, axis, pairs)]
    pallas_call x5, Pallas kernels: 8.48 us -> 8.99 us  [call(): pl.pallas_call(kernel, out_shape=shapes, in_specs=[specs[k] for k, _ in a...]
  transfers between devices with their start and end apart: 6 -> 6, of which waited for: 1 -> 1; matrix products, arithmetic and copies ran while one was open for 0% -> 0% of each run, Pallas kernels for 25% -> 28%
where the time goes in v7:
time: 21.7 us; the launch traced here: 21.3 us
  starting transfers between devices  10.5 us (48%)
  Pallas kernels  8.99 us (41%)
  between operations  1.35 us (6%)
  waiting for transfers between devices  0.4 us (2%)
    pallas_call x5, Pallas kernels, call(): pl.pallas_call(kernel, out_shape=shapes, in_specs=[specs[k] for k, _ in a...  8.99 us
    ppermute x2, starting transfers between devices, moved(): lax.ppermute(array, axis, [(i, (i + step) % peers) for i in range(peers)])  6.47 us
    ppermute x4, starting transfers between devices, swapped(): return lax.ppermute(array, axis, pairs)  4.06 us
  transfers between devices with their start and end apart: 6, of which 1 were waited for; matrix products, arithmetic and copies ran while one was open for 0% of the time, Pallas kernels for 28%

profile of v7, /device:TPU:0, one launch (start us, length us, event | category | flops | bytes accessed | tf_op | source)
XLA Modules:
  0.0 21.3 jit_solution(18277764356889973732)
XLA Ops:
  0.6 2.0 %pack.1 = (f32[14,32,128]{2,1,0:T(8,128)S(1)}, f32[14,32,128]{2,1,0:T(8,128)S(1)}, f32[272,128]{1,0:T(8,128)S(1)}, f32[272,128]{1,0:T(8,128)S(1)}, f32[3,40,48,1...) custom-call(f32[3,32,32,128]{3,2,1,0:T(8,128)} %vel.1, f32[32,32,128]{2,1,0:T(8,128)} %press.3, ...), custom_call_target="tpu_custom_call" | custom-call | flops 1048576 | bytes 4194304 | tf_op jit(solution)/shard_map/pack/pallas_call | solution.py:40
  2.7 1.6 %collective-permute-start.2 = (f32[272,128]{1,0:T(8,128)S(1)}, f32[272,128]{1,0:T(8,128)S(1)}, u32[]{:S(2)}, u32[]{:S(2)}) collective-permute-start(f32[272,128]{1,0:T(8,128)S(1)} %get-tuple-element.36), channel_id=1, source_target_pairs={{0,1},{1,2},{2,3},{3,4},{4,5},{5,6},{6,7},{7,8},{8,9},{9,10},{10,1... | collective-permute-start | bytes 417800 | tf_op jit(solution)/shard_map/ppermute | solution.py:426
  4.3 4.8 %collective-permute-start.3 = (f32[272,128]{1,0:T(8,128)S(1)}, f32[272,128]{1,0:T(8,128)S(1)}, u32[]{:S(2)}, u32[]{:S(2)}) collective-permute-start(f32[272,128]{1,0:T(8,128)S(1)} %get-tuple-element.37), channel_id=1, source_target_pairs={{0,15},{1,0},{2,1},{3,2},{4,3},{5,4},{6,5},{7,6},{8,7},{9,8},{10,9... | collective-permute-start | bytes 417800 | tf_op jit(solution)/shard_map/ppermute | solution.py:426
  9.1 0.0 collective-permute-start
  9.1 3.1 %collective-permute-start.1 = (f32[14,32,128]{2,1,0:T(8,128)S(1)}, f32[14,32,128]{2,1,0:T(8,128)S(1)}, u32[]{:S(2)}, u32[]{:S(2)}) collective-permute-start(f32[14,32,128]{2,1,0:T(8,128)S(1)} %get-tuple-element.35), channel_id=1, source_target_pairs={{0,112},{16,32},{32,16},{48,64},{64,48},{80,96},{96,80},{112,0},{1... | collective-permute-start | bytes 688136 | tf_op jit(solution)/shard_map/ppermute | solution.py:432
  12.9 2.4 %inner.1 = (f32[40,48,128]{2,1,0:T(8,128)S(1)}, s32[32,32,128]{2,1,0:T(8,128)S(1)}, f32[3,32,32,128]{3,2,1,0:T(8,128)S(1)}, f32[40,48,128]{2,1,0:T(8,128)S(1)}, ...) custom-call(f32[3,40,48,128]{3,2,1,0:T(8,128)S(1)} %get-tuple-elemen, ...), custom_call_target="tpu_custom_call", output_to_operand_aliasing={{0}: (6, {})} | custom-call | flops 4026531840 | bytes 4194304 | tf_op jit(solution)/shard_map/inner/pallas_call | solution.py:40
  15.3 0.0 collective-permute-done.2.q_lo
  15.3 0.0 collective-permute-done.3.q_hi
  15.4 0.1 relay.1
  15.5 0.1 collective-permute-start.4
  15.6 0.8 %collective-permute-start.5 = (f32[2,32,128]{2,1,0:T(8,128)S(1)}, f32[2,32,128]{2,1,0:T(8,128)S(1)}, u32[]{:S(2)}, u32[]{:S(2)}) collective-permute-start(f32[2,32,128]{2,1,0:T(8,128)S(1)} %get-tuple-element.47), channel_id=1, source_target_pairs={{0,112},{16,32},{32,16},{48,64},{64,48},{80,96},{96,80},{112,0},{1... | collective-permute-start | bytes 98312 | tf_op jit(solution)/shard_map/ppermute | solution.py:432
  16.4 0.0 collective-permute-done.x_in
  16.4 0.0 collective-permute-done.1.x_out
  16.4 3.4 %edge.1 = (f32[3,40,48,128]{3,2,1,0:T(8,128)S(1)}, f32[40,48,128]{2,1,0:T(8,128)S(1)}, f32[40,48,128]{2,1,0:T(8,128)S(1)}, f32[3,32,32,128]{3,2,1,0:T(8,128)S(1)...) custom-call(s32[32,32,128]{2,1,0:T(8,128)S(1)} %get-tuple-element.32, ...), custom_call_target="tpu_custom_call", output_to_operand_aliasing={{0}: (6, {}), {1}: (7, {}), {2}: (8, {}), {3}: (9, {}), {4}... | custom-call | flops 4026531840 | bytes 4194304 | tf_op jit(solution)/shard_map/edge/pallas_call | solution.py:40
  19.8 0.0 collective-permute-done.4.z_in
  19.8 0.4 %collective-permute-done.5.z_out = f32[2,32,128]{2,1,0:T(8,128)S(1)} collective-permute-done((f32[2,32,128]{2,1,0:T(8,128)S(1)}, f32[2,32,128]{2,1,0:T(8,128)S(1)}, u32[]{:S(2)}, u32[]{:S(2)}) %collective-permute-start.5) | collective-permute-done | bytes 32800 | tf_op jit(solution)/shard_map/ppermute | solution.py:432
  20.2 1.0 %corner.1 = (f32[3,40,48,128]{3,2,1,0:T(8,128)S(1)}, f32[40,48,128]{2,1,0:T(8,128)S(1)}, f32[40,48,128]{2,1,0:T(8,128)S(1)}, f32[40,48,128]{2,1,0:T(8,128)S(1)},...) custom-call(f32[4,8,128]{2,1,0:T(8,128)S(1)} %get-tuple-element.33.M, ...), custom_call_target="tpu_custom_call", output_to_operand_aliasing={{0}: (3, {}), {1}: (4, {}), {2}: (5, {}), {3}: (6, {}), {4}... | custom-call | flops 1048576 | bytes 4194304 | tf_op jit(solution)/shard_map/corner/pallas_call | solution.py:40
Async XLA Ops:
  2.7 12.7 %collective-permute-start.2 = (f32[272,128]{1,0:T(8,128)S(1)}, f32[272,128]{1,0:T(8,128)S(1)}, u32[]{:S(2)}, u32[]{:S(2)}) collective-permute-start(f32[272,128]{1,0:T(8,128)S(1)} %get-tuple-element.36), channel_id=1, source_target_pairs={{0,1},{1,2},{2,3},{3,4},{4,5},{5,6},{6,7},{7,8},{8,9},{9,10},{10,1... | collective-permute-start | bytes 417800 | tf_op jit(solution)/shard_map/ppermute | solution.py:426
  4.3 11.0 %collective-permute-start.3 = (f32[272,128]{1,0:T(8,128)S(1)}, f32[272,128]{1,0:T(8,128)S(1)}, u32[]{:S(2)}, u32[]{:S(2)}) collective-permute-start(f32[272,128]{1,0:T(8,128)S(1)} %get-tuple-element.37), channel_id=1, source_target_pairs={{0,15},{1,0},{2,1},{3,2},{4,3},{5,4},{6,5},{7,6},{8,7},{9,8},{10,9... | collective-permute-start | bytes 417800 | tf_op jit(solution)/shard_map/ppermute | solution.py:426
  9.1 7.3 %collective-permute-start = (f32[14,32,128]{2,1,0:T(8,128)S(1)}, f32[14,32,128]{2,1,0:T(8,128)S(1)}, u32[]{:S(2)}, u32[]{:S(2)}) collective-permute-start(f32[14,32,128]{2,1,0:T(8,128)S(1)} %get-tuple-element.34), channel_id=1, source_target_pairs={{0,16},{16,0},{32,48},{48,32},{64,80},{80,64},{96,112},{112,96},{1... | collective-permute-start | bytes 688136 | tf_op jit(solution)/shard_map/ppermute | solution.py:432
  9.1 7.3 %collective-permute-start.1 = (f32[14,32,128]{2,1,0:T(8,128)S(1)}, f32[14,32,128]{2,1,0:T(8,128)S(1)}, u32[]{:S(2)}, u32[]{:S(2)}) collective-permute-start(f32[14,32,128]{2,1,0:T(8,128)S(1)} %get-tuple-element.35), channel_id=1, source_target_pairs={{0,112},{16,32},{32,16},{48,64},{64,48},{80,96},{96,80},{112,0},{1... | collective-permute-start | bytes 688136 | tf_op jit(solution)/shard_map/ppermute | solution.py:432
  15.5 4.3 %collective-permute-start.4 = (f32[2,32,128]{2,1,0:T(8,128)S(1)}, f32[2,32,128]{2,1,0:T(8,128)S(1)}, u32[]{:S(2)}, u32[]{:S(2)}) collective-permute-start(f32[2,32,128]{2,1,0:T(8,128)S(1)} %get-tuple-element.46), channel_id=1, source_target_pairs={{0,16},{16,0},{32,48},{48,32},{64,80},{80,64},{96,112},{112,96},{1... | collective-permute-start | bytes 98312 | tf_op jit(solution)/shard_map/ppermute | solution.py:432
  15.6 4.6 %collective-permute-start.5 = (f32[2,32,128]{2,1,0:T(8,128)S(1)}, f32[2,32,128]{2,1,0:T(8,128)S(1)}, u32[]{:S(2)}, u32[]{:S(2)}) collective-permute-start(f32[2,32,128]{2,1,0:T(8,128)S(1)} %get-tuple-element.47), channel_id=1, source_target_pairs={{0,112},{16,32},{32,16},{48,64},{64,48},{80,96},{96,80},{112,0},{1... | collective-permute-start | bytes 98312 | tf_op jit(solution)/shard_map/ppermute | solution.py:432
